TPU v7x, 128 devices: a whole 4x4x4 slice. The times are simulated.
128 devices in a mesh: stn: 16 (over y_lo, z, core), chan: 8 (over x, y_hi).
Axes of the slice: x: 4, y: 4 (y_hi: 2, y_lo: 2; y = y_hi * 2 + y_lo), z: 4, core: 2. Of those that a mesh axis runs over, the one named last changes fastest.
Arguments:
- voltages: bfloat16 [2, 1024, 253952], P(None, ('stn', 'chan')), may hold values from -6 to 6
- filter_taps: float32 [16, 8192], replicated, may hold values from -1.5 to 1.5
- station_flags: int32 [512], P(('stn', 'chan')), may hold values 0 or 1
- subband_lists: int32 [8, 16], replicated, may hold values from 0 to 2047, as said below
- subband_counts: int32 [8], replicated, may hold values from 1 to 16, as said below
Outputs:
- visibilities: float32 [16, 9, 512, 64, 128], P('stn', None, 'chan')
Inputs may be any that keep to these rules, and one draw needn't show every extreme that they name: `subband_lists`: each entry names a subband of 4 channels; all 8 x 16 entries differ. Group g uses the subbands of its first subband_counts[g] slots; the other slots are not used.
All inputs are finite; a program needn't handle non-finite values. No bound on the sum of `station_flags` on one device may be relied on, other than what follows from the above.
Results may differ from a plain program's by a relative error of at most 0.0083.
Values may be sent and summed in bfloat16 or wider, within the bound.
No kernel may reach another device: no remote copies, remote signals or barrier semaphores. Data moves between devices by JAX's collectives and lax.ppermute only.
A program may use at most 192 MiB of HBM per device.

v0:
```python
import math

import jax
import jax.numpy as jnp
from jax import lax
from jax.sharding import PartitionSpec as P

NCH = 8192
FIRST = 64
SECOND = 128
TAPS = 16
SPECTRA = 16
SUBW = 4


def shifted(array, axis, by):
    length = lax.axis_size(axis)
    return lax.ppermute(array, axis, [(i, (i + by) % length) for i in range(length)])


def cosine_tables(length):
    indices = jnp.arange(length, dtype=jnp.int32)
    products = indices[:, None] * indices[None, :] % length
    angles = products.astype(jnp.float32) * (2.0 * math.pi / length)
    return (jnp.cos(angles).astype(jnp.bfloat16), jnp.sin(angles).astype(jnp.bfloat16))


def twiddles():
    row_index = jnp.arange(FIRST, dtype=jnp.int32)
    col_index = jnp.arange(SECOND, dtype=jnp.int32)
    products = row_index[:, None] * col_index[None, :] % NCH
    angles = products.astype(jnp.float32) * (2.0 * math.pi / NCH)
    return (jnp.cos(angles), jnp.sin(angles))


def selection_tables(channel_ids):
    flat_index = jnp.arange(NCH, dtype=jnp.int32)
    row_k = flat_index // SECOND
    row_b = flat_index % SECOND
    chosen_k = channel_ids % FIRST
    chosen_m = channel_ids // FIRST
    products = row_b[:, None] * chosen_m[None, :] % SECOND
    angles = products.astype(jnp.float32) * (2.0 * math.pi / SECOND)
    member = (row_k[:, None] == chosen_k[None, :]).astype(jnp.bfloat16)
    return (
        jnp.cos(angles).astype(jnp.bfloat16) * member,
        jnp.sin(angles).astype(jnp.bfloat16) * member,
    )


def correlate(local_block, others, half):
    local_real = local_block[..., :half]
    local_imag = local_block[..., half:]
    other_real = others[..., :half]
    other_imag = others[..., half:]
    form = "fta,...ftb->...fab"
    real_part = jnp.einsum(
        form, local_real, other_real, preferred_element_type=jnp.float32
    ) + jnp.einsum(form, local_imag, other_imag, preferred_element_type=jnp.float32)
    imag_part = jnp.einsum(
        form, local_imag, other_real, preferred_element_type=jnp.float32
    ) - jnp.einsum(form, local_real, other_imag, preferred_element_type=jnp.float32)
    return jnp.concatenate([real_part, imag_part], axis=-1)


def per_device(voltages, filter_taps, station_flags, subband_lists, subband_counts):
    n_stn = lax.axis_size("stn")
    local_inputs = voltages.shape[1]
    cosine_first, sine_first = cosine_tables(FIRST)
    twiddle_cos, twiddle_sin = twiddles()
    offsets = jnp.arange(SUBW, dtype=jnp.int32)
    channel_ids = (subband_lists[:, :, None] * SUBW + offsets[None, None, :]).reshape(-1)
    select_cos, select_sin = selection_tables(channel_ids)
    input_flags = jnp.repeat(station_flags, 2).astype(jnp.float32)
    scale = input_flags / math.sqrt(NCH)
    segments = voltages.reshape(2, local_inputs, SPECTRA + TAPS - 1, NCH)

    def tap_step(offset, frame):
        piece = lax.dynamic_slice_in_dim(segments, offset, SPECTRA, 2)
        coeffs = lax.dynamic_index_in_dim(filter_taps, offset, 0, keepdims=False)
        return frame + coeffs * piece.astype(jnp.float32)

    frame = lax.fori_loop(
        0, TAPS, tap_step, jnp.zeros((2, local_inputs, SPECTRA, NCH), jnp.float32)
    )
    frame = frame.astype(jnp.bfloat16).reshape(2, local_inputs, SPECTRA, FIRST, SECOND)
    form_one = "ltab,ak->ltkb"
    first_real = jnp.einsum(
        form_one, frame[0], cosine_first, preferred_element_type=jnp.float32
    ) + jnp.einsum(form_one, frame[1], sine_first, preferred_element_type=jnp.float32)
    first_imag = jnp.einsum(
        form_one, frame[1], cosine_first, preferred_element_type=jnp.float32
    ) - jnp.einsum(form_one, frame[0], sine_first, preferred_element_type=jnp.float32)
    rotated_real = (
        (first_real * twiddle_cos + first_imag * twiddle_sin)
        .astype(jnp.bfloat16)
        .reshape(local_inputs, SPECTRA, NCH)
    )
    rotated_imag = (
        (first_imag * twiddle_cos - first_real * twiddle_sin)
        .astype(jnp.bfloat16)
        .reshape(local_inputs, SPECTRA, NCH)
    )
    form_two = "ltx,xc->ctl"
    spec_real = (
        jnp.einsum(form_two, rotated_real, select_cos, preferred_element_type=jnp.float32)
        + jnp.einsum(form_two, rotated_imag, select_sin, preferred_element_type=jnp.float32)
    ) * scale
    spec_imag = (
        jnp.einsum(form_two, rotated_imag, select_cos, preferred_element_type=jnp.float32)
        - jnp.einsum(form_two, rotated_real, select_sin, preferred_element_type=jnp.float32)
    ) * scale
    selected = jnp.stack([spec_real, spec_imag], axis=2).astype(jnp.bfloat16)
    received = lax.all_to_all(selected, "chan", split_axis=0, concat_axis=3, tiled=True)
    half = received.shape[3]
    slots = received.shape[0]
    local_block = received.reshape(slots, SPECTRA, 2 * half)
    group = lax.axis_index("chan")
    group_count = lax.dynamic_index_in_dim(subband_counts, group, 0, keepdims=False)
    slot_index = jnp.arange(slots, dtype=jnp.int32)
    live_slots = (slot_index // SUBW < group_count).astype(jnp.float32) / SPECTRA
    distances = n_stn // 2 + 1
    nearest = correlate(local_block, local_block, half)

    def advance(moving, unused):
        moving = shifted(moving, "stn", -1)
        return (moving, correlate(local_block, moving, half))

    moving, further = lax.scan(advance, local_block, None, length=distances - 1)
    result = jnp.concatenate([nearest[None], further], axis=0)
    result = result * live_slots[None, :, None, None]
    return result[None]


def solution(mesh):
    placed = (P(None, ("stn", "chan"), None), P(), P(("stn", "chan")), P(), P())
    return jax.shard_map(
        per_device,
        mesh=mesh,
        in_specs=placed,
        out_specs=P("stn", None, "chan", None, None),
        check_vma=False,
    )
```

profile of v0, /device:TPU:97, one launch (start us, length us, event | category | flops | bytes accessed | tf_op | source)
XLA Modules:
  0.0 686.0 jit_solution(11161933933146433922)
XLA Ops:
  0.2 261.9 %while.27 = (s32[]{:T(128)}, f32[2,8,16,8192]{3,2,1,0:T(8,128)}, f32[16,8192]{1,0:T(8,128)}, bf16[2,8,31,8192]{3,1,2,0:T(8,128)(2,1)}, s32[]{:T(128)}, /*index=5*/s32[]{:T(128)}) while((s32[]{:T(128)}, f32[2,8,16,8192]{3,2,1,0:T(8,128)}, f32[16,8192]{1,0:T(8,128)}, bf16[2,8,31,8192]{3,1,2,0:T(8,128)(2,1)}, s32[]{:T(128)}, ...), condition=%wide.region_1.2_spmd.clone, body=%wide.region_0.1_spmd.clone.sunk | while | flops 8388611 | bytes 29458524 | solution.py:83
  5.7 8.6 %select_add_fusion.2 = f32[2,8,16,8192]{3,2,1,0:T(8,128)} fusion(f32[2,8,16,8192]{3,2,1,0:T(8,128)} %get-tuple-element.222, bf16[2,8,16,8192]{3,1,2,0:T(8,128)(2,1)} %constant_dynamic-slice_fusion.4, f32[8192]{0:T(1024)S(1)} %bitcast.127, pred[]{:T(512)S(6)} %compare.31), kind=kLoop, calls=%fused_computation.14.clone.1 | loop fusion | flops 8388608 | bytes 21004288 | tf_op jit(solution)/shard_map/while/body/eval_jaxpr/add | solution.py:81
  19.9 11.0 %select_add_fusion.2 = f32[2,8,16,8192]{3,2,1,0:T(8,128)} fusion(f32[2,8,16,8192]{3,2,1,0:T(8,128)} %get-tuple-element.222, bf16[2,8,16,8192]{3,1,2,0:T(8,128)(2,1)} %constant_dynamic-slice_fusion.4, f32[8192]{0:T(1024)S(1)} %bitcast.127, pred[]{:T(512)S(6)} %compare.31), kind=kLoop, calls=%fused_computation.14.clone.1 | loop fusion | flops 8388608 | bytes 21004288 | tf_op jit(solution)/shard_map/while/body/eval_jaxpr/add | solution.py:81
  36.4 11.0 %select_add_fusion.2 = f32[2,8,16,8192]{3,2,1,0:T(8,128)} fusion(f32[2,8,16,8192]{3,2,1,0:T(8,128)} %get-tuple-element.222, bf16[2,8,16,8192]{3,1,2,0:T(8,128)(2,1)} %constant_dynamic-slice_fusion.4, f32[8192]{0:T(1024)S(1)} %bitcast.127, pred[]{:T(512)S(6)} %compare.31), kind=kLoop, calls=%fused_computation.14.clone.1 | loop fusion | flops 8388608 | bytes 21004288 | tf_op jit(solution)/shard_map/while/body/eval_jaxpr/add | solution.py:81
  52.9 11.0 %select_add_fusion.2 = f32[2,8,16,8192]{3,2,1,0:T(8,128)} fusion(f32[2,8,16,8192]{3,2,1,0:T(8,128)} %get-tuple-element.222, bf16[2,8,16,8192]{3,1,2,0:T(8,128)(2,1)} %constant_dynamic-slice_fusion.4, f32[8192]{0:T(1024)S(1)} %bitcast.127, pred[]{:T(512)S(6)} %compare.31), kind=kLoop, calls=%fused_computation.14.clone.1 | loop fusion | flops 8388608 | bytes 21004288 | tf_op jit(solution)/shard_map/while/body/eval_jaxpr/add | solution.py:81
  69.4 11.0 %select_add_fusion.2 = f32[2,8,16,8192]{3,2,1,0:T(8,128)} fusion(f32[2,8,16,8192]{3,2,1,0:T(8,128)} %get-tuple-element.222, bf16[2,8,16,8192]{3,1,2,0:T(8,128)(2,1)} %constant_dynamic-slice_fusion.4, f32[8192]{0:T(1024)S(1)} %bitcast.127, pred[]{:T(512)S(6)} %compare.31), kind=kLoop, calls=%fused_computation.14.clone.1 | loop fusion | flops 8388608 | bytes 21004288 | tf_op jit(solution)/shard_map/while/body/eval_jaxpr/add | solution.py:81
  85.9 11.0 %select_add_fusion.2 = f32[2,8,16,8192]{3,2,1,0:T(8,128)} fusion(f32[2,8,16,8192]{3,2,1,0:T(8,128)} %get-tuple-element.222, bf16[2,8,16,8192]{3,1,2,0:T(8,128)(2,1)} %constant_dynamic-slice_fusion.4, f32[8192]{0:T(1024)S(1)} %bitcast.127, pred[]{:T(512)S(6)} %compare.31), kind=kLoop, calls=%fused_computation.14.clone.1 | loop fusion | flops 8388608 | bytes 21004288 | tf_op jit(solution)/shard_map/while/body/eval_jaxpr/add | solution.py:81
  102.5 11.0 %select_add_fusion.2 = f32[2,8,16,8192]{3,2,1,0:T(8,128)} fusion(f32[2,8,16,8192]{3,2,1,0:T(8,128)} %get-tuple-element.222, bf16[2,8,16,8192]{3,1,2,0:T(8,128)(2,1)} %constant_dynamic-slice_fusion.4, f32[8192]{0:T(1024)S(1)} %bitcast.127, pred[]{:T(512)S(6)} %compare.31), kind=kLoop, calls=%fused_computation.14.clone.1 | loop fusion | flops 8388608 | bytes 21004288 | tf_op jit(solution)/shard_map/while/body/eval_jaxpr/add | solution.py:81
  119.0 11.0 %select_add_fusion.2 = f32[2,8,16,8192]{3,2,1,0:T(8,128)} fusion(f32[2,8,16,8192]{3,2,1,0:T(8,128)} %get-tuple-element.222, bf16[2,8,16,8192]{3,1,2,0:T(8,128)(2,1)} %constant_dynamic-slice_fusion.4, f32[8192]{0:T(1024)S(1)} %bitcast.127, pred[]{:T(512)S(6)} %compare.31), kind=kLoop, calls=%fused_computation.14.clone.1 | loop fusion | flops 8388608 | bytes 21004288 | tf_op jit(solution)/shard_map/while/body/eval_jaxpr/add | solution.py:81
  135.5 11.0 %select_add_fusion.2 = f32[2,8,16,8192]{3,2,1,0:T(8,128)} fusion(f32[2,8,16,8192]{3,2,1,0:T(8,128)} %get-tuple-element.222, bf16[2,8,16,8192]{3,1,2,0:T(8,128)(2,1)} %constant_dynamic-slice_fusion.4, f32[8192]{0:T(1024)S(1)} %bitcast.127, pred[]{:T(512)S(6)} %compare.31), kind=kLoop, calls=%fused_computation.14.clone.1 | loop fusion | flops 8388608 | bytes 21004288 | tf_op jit(solution)/shard_map/while/body/eval_jaxpr/add | solution.py:81
  152.0 11.0 %select_add_fusion.2 = f32[2,8,16,8192]{3,2,1,0:T(8,128)} fusion(f32[2,8,16,8192]{3,2,1,0:T(8,128)} %get-tuple-element.222, bf16[2,8,16,8192]{3,1,2,0:T(8,128)(2,1)} %constant_dynamic-slice_fusion.4, f32[8192]{0:T(1024)S(1)} %bitcast.127, pred[]{:T(512)S(6)} %compare.31), kind=kLoop, calls=%fused_computation.14.clone.1 | loop fusion | flops 8388608 | bytes 21004288 | tf_op jit(solution)/shard_map/while/body/eval_jaxpr/add | solution.py:81
  168.5 11.0 %select_add_fusion.2 = f32[2,8,16,8192]{3,2,1,0:T(8,128)} fusion(f32[2,8,16,8192]{3,2,1,0:T(8,128)} %get-tuple-element.222, bf16[2,8,16,8192]{3,1,2,0:T(8,128)(2,1)} %constant_dynamic-slice_fusion.4, f32[8192]{0:T(1024)S(1)} %bitcast.127, pred[]{:T(512)S(6)} %compare.31), kind=kLoop, calls=%fused_computation.14.clone.1 | loop fusion | flops 8388608 | bytes 21004288 | tf_op jit(solution)/shard_map/while/body/eval_jaxpr/add | solution.py:81
  185.1 11.0 %select_add_fusion.2 = f32[2,8,16,8192]{3,2,1,0:T(8,128)} fusion(f32[2,8,16,8192]{3,2,1,0:T(8,128)} %get-tuple-element.222, bf16[2,8,16,8192]{3,1,2,0:T(8,128)(2,1)} %constant_dynamic-slice_fusion.4, f32[8192]{0:T(1024)S(1)} %bitcast.127, pred[]{:T(512)S(6)} %compare.31), kind=kLoop, calls=%fused_computation.14.clone.1 | loop fusion | flops 8388608 | bytes 21004288 | tf_op jit(solution)/shard_map/while/body/eval_jaxpr/add | solution.py:81
  201.6 11.0 %select_add_fusion.2 = f32[2,8,16,8192]{3,2,1,0:T(8,128)} fusion(f32[2,8,16,8192]{3,2,1,0:T(8,128)} %get-tuple-element.222, bf16[2,8,16,8192]{3,1,2,0:T(8,128)(2,1)} %constant_dynamic-slice_fusion.4, f32[8192]{0:T(1024)S(1)} %bitcast.127, pred[]{:T(512)S(6)} %compare.31), kind=kLoop, calls=%fused_computation.14.clone.1 | loop fusion | flops 8388608 | bytes 21004288 | tf_op jit(solution)/shard_map/while/body/eval_jaxpr/add | solution.py:81
  218.1 11.0 %select_add_fusion.2 = f32[2,8,16,8192]{3,2,1,0:T(8,128)} fusion(f32[2,8,16,8192]{3,2,1,0:T(8,128)} %get-tuple-element.222, bf16[2,8,16,8192]{3,1,2,0:T(8,128)(2,1)} %constant_dynamic-slice_fusion.4, f32[8192]{0:T(1024)S(1)} %bitcast.127, pred[]{:T(512)S(6)} %compare.31), kind=kLoop, calls=%fused_computation.14.clone.1 | loop fusion | flops 8388608 | bytes 21004288 | tf_op jit(solution)/shard_map/while/body/eval_jaxpr/add | solution.py:81
  234.6 11.0 %select_add_fusion.2 = f32[2,8,16,8192]{3,2,1,0:T(8,128)} fusion(f32[2,8,16,8192]{3,2,1,0:T(8,128)} %get-tuple-element.222, bf16[2,8,16,8192]{3,1,2,0:T(8,128)(2,1)} %constant_dynamic-slice_fusion.4, f32[8192]{0:T(1024)S(1)} %bitcast.127, pred[]{:T(512)S(6)} %compare.31), kind=kLoop, calls=%fused_computation.14.clone.1 | loop fusion | flops 8388608 | bytes 21004288 | tf_op jit(solution)/shard_map/while/body/eval_jaxpr/add | solution.py:81
  251.1 11.0 %select_add_fusion.2 = f32[2,8,16,8192]{3,2,1,0:T(8,128)} fusion(f32[2,8,16,8192]{3,2,1,0:T(8,128)} %get-tuple-element.222, bf16[2,8,16,8192]{3,1,2,0:T(8,128)(2,1)} %constant_dynamic-slice_fusion.4, f32[8192]{0:T(1024)S(1)} %bitcast.127, pred[]{:T(512)S(6)} %compare.31), kind=kLoop, calls=%fused_computation.14.clone.1 | loop fusion | flops 8388608 | bytes 21004288 | tf_op jit(solution)/shard_map/while/body/eval_jaxpr/add | solution.py:81
  280.5 71.1 %fusion.16 = f32[512,8,16]{0,2,1:T(8,128)S(1)} fusion(bf16[8,16,8192]{2,1,0:T(8,128)(2,1)} %reshape.181, s32[512]{0:T(512)S(1)} %get-tuple-element.160, s32[8192]{0:T(1024)S(1)} %get-tuple-element.163, s32[512]{0:T(512)S(1)} %get-tuple-element.159, s32[8192]{0:T(1024)S(1)} %get-tuple-element.164), kind=kOutput, calls=%fused_computation.32 | convolution fusion | flops 1145044992 | bytes 2428928 | tf_op jit(solution)/shard_map/ltx,xc->ctl/dot_general | solution.py:111
  351.6 64.2 %fusion.18 = f32[512,8,16]{0,2,1:T(8,128)S(1)} fusion(bf16[8,16,8192]{2,1,0:T(8,128)(2,1)S(1)} %copy-done.1, s32[512]{0:T(512)S(1)} %get-tuple-element.160, s32[8192]{0:T(1024)S(1)} %get-tuple-element.163, s32[512]{0:T(512)S(1)} %get-tuple-element.159, s32[8192]{0:T(1024)S(1)} %get-tuple-element.164), kind=kOutput, calls=%fused_computation.33 | convolution fusion | flops 1145044992 | bytes 2428928 | tf_op jit(solution)/shard_map/ltx,xc->ctl/dot_general | solution.py:107
  415.8 63.4 %fusion.57 = bf16[512,16,1,8]{0,1,3,2:T(8,128)(2,1)S(1)} fusion(f32[512,8,16]{0,2,1:T(8,128)S(1)} %fusion.16, bf16[8,16,8192]{2,1,0:T(8,128)(2,1)S(1)} %copy-done.1, s32[512]{0:T(512)S(1)} %get-tuple-element.160, s32[8192]{0:T(1024)S(1)} %get-tuple-element.163, s32[512]{0:T(512)S(1)} %get-tuple-element.159, s32[8192]{0:T(1024)S(1)} %get-tuple-element.164, ...), kind=kOutput, calls=%fused_computation.62 | convolution fusion | flops 1145241600 | bytes 2560032 | tf_op jit(solution)/shard_map/ltx,xc->ctl/dot_general | solution.py:110
  479.2 63.2 %fusion.54 = bf16[512,16,1,8]{0,1,3,2:T(8,128)(2,1)S(1)} fusion(f32[512,8,16]{0,2,1:T(8,128)S(1)} %fusion.18, bf16[8,16,8192]{2,1,0:T(8,128)(2,1)S(1)} %copy-done, s32[512]{0:T(512)S(1)} %get-tuple-element.160, s32[8192]{0:T(1024)S(1)} %get-tuple-element.163, s32[512]{0:T(512)S(1)} %get-tuple-element.159, s32[8192]{0:T(1024)S(1)} %get-tuple-element.164, ...), kind=kOutput, calls=%fused_computation.61 | convolution fusion | flops 1145241600 | bytes 2560032 | tf_op jit(solution)/shard_map/ltx,xc->ctl/dot_general | solution.py:106
  568.4 102.6 %while.26 = (s32[]{:T(128)}, bf16[64,16,128]{2,1,0:T(8,128)(2,1)S(1)}, f32[8,64,64,128]{3,2,1,0:T(8,128)}, bf16[64,16,128]{2,1,0:T(8,128)(2,1)S(1)}, s32[]{:T(128)}) while((s32[]{:T(128)}, bf16[64,16,128]{2,1,0:T(8,128)(2,1)S(1)}, f32[8,64,64,128]{3,2,1,0:T(8,128)}, bf16[64,16,128]{2,1,0:T(8,128)(2,1)S(1)}, s32[]{:T(128)}) %tuple.57), condition=%wide.region_3.4_spmd, body=%wide.region_2.3_spmd.sunk | while | flops 34603008 | bytes 14155889 | solution.py:129
  581.3 7.9 %collective-permute-done = bf16[64,16,128]{2,1,0:T(8,128)(2,1)S(1)} collective-permute-done((bf16[64,16,128]{2,1,0:T(8,128)(2,1)S(1)}, bf16[64,16,128]{2,1,0:T(8,128)(2,1)S(1)}, u32[]{:S(2)}, u32[]{:S(2)}) %collective-permute-start) | collective-permute-done | bytes 262176 | tf_op jit(solution)/shard_map/while/body/eval_jaxpr/ppermute | solution.py:18
  671.0 14.8 %maximum_multiply_fusion = f32[1,9,64,64,128]{4,3,2,1,0:T(8,128)} fusion(f32[1,8,64,64,128]{4,3,2,1,0:T(8,128)} %bitcast.122, f32[1,1,64,64,128]{4,3,2,1,0:T(8,128)S(1)} %maximum_bitcast_fusion.1, f32[64]{0:T(128)S(1)} %compare_select_fusion.2), kind=kLoop, calls=%fused_computation.24 | loop fusion | flops 9437184 | bytes 37748992 | tf_op jit(solution)/shard_map/mul | solution.py:131
  (142 shorter events, 227.6 us)
Async XLA Ops:
  270.3 7.5 %copy-start.2 = (s32[8,16]{1,0:T(8,128)S(1)}, s32[8,16]{1,0:T(8,128)}, u32[]{:S(2)}) copy-start(s32[8,16]{1,0:T(8,128)} %param.12) | copy-start | bytes 1540
  270.4 10.0 %copy-start.3 = (s32[4]{0:T(128)S(1)}, s32[4]{0:T(128)}, u32[]{:S(2)}) copy-start(s32[4]{0:T(128)} %param.11) | copy-start | bytes 52
  280.5 71.1 %copy-start.1 = (bf16[8,16,8192]{2,1,0:T(8,128)(2,1)S(1)}, bf16[8,16,8192]{2,1,0:T(8,128)(2,1)}, u32[]{:S(2)}) copy-start(bf16[8,16,8192]{2,1,0:T(8,128)(2,1)} %reshape.182) | copy-start | bytes 6291460
  415.7 63.4 %copy-start = (bf16[8,16,8192]{2,1,0:T(8,128)(2,1)S(1)}, bf16[8,16,8192]{2,1,0:T(8,128)(2,1)}, u32[]{:S(2)}) copy-start(bf16[8,16,8192]{2,1,0:T(8,128)(2,1)} %reshape.181) | copy-start | bytes 6291460
  479.2 74.7 %copy-start.4 = (s32[8]{0:T(128)S(1)}, s32[8]{0:T(128)}, u32[]{:S(2)}) copy-start(s32[8]{0:T(128)} %param.13) | copy-start | bytes 100
  547.2 14.1 %all-to-all-start = ((bf16[8,2,8192]{2,1,0:T(2,128)(2,1)}), bf16[8,2,8192]{2,1,0:T(2,128)(2,1)S(1)}, u32[]{:S(2)}, u32[]{:S(2)}) async-start(bf16[8,2,8192]{2,1,0:T(2,128)(2,1)} %reshape.188), calls=%async_computation | async-start | bytes 524288 | tf_op jit(solution)/shard_map/all_to_all | solution.py:114
  568.4 8.0 %collective-permute-start = (bf16[64,16,128]{2,1,0:T(8,128)(2,1)S(1)}, bf16[64,16,128]{2,1,0:T(8,128)(2,1)S(1)}, u32[]{:S(2)}, u32[]{:S(2)}) collective-permute-start(bf16[64,16,128]{2,1,0:T(8,128)(2,1)S(1)} %get-tuple-element.239), channel_id=1, source_target_pairs={{0,120},{8,0},{16,8},{24,16},{32,24},{40,32},{48,40},{56,48},{64,5... | collective-permute-start | bytes 786440 | tf_op jit(solution)/shard_map/while/body/eval_jaxpr/ppermute | solution.py:18
  581.2 8.0 %collective-permute-start = (bf16[64,16,128]{2,1,0:T(8,128)(2,1)S(1)}, bf16[64,16,128]{2,1,0:T(8,128)(2,1)S(1)}, u32[]{:S(2)}, u32[]{:S(2)}) collective-permute-start(bf16[64,16,128]{2,1,0:T(8,128)(2,1)S(1)} %get-tuple-element.239), channel_id=1, source_target_pairs={{0,120},{8,0},{16,8},{24,16},{32,24},{40,32},{48,40},{56,48},{64,5... | collective-permute-start | bytes 786440 | tf_op jit(solution)/shard_map/while/body/eval_jaxpr/ppermute | solution.py:18
  594.0 8.0 %collective-permute-start = (bf16[64,16,128]{2,1,0:T(8,128)(2,1)S(1)}, bf16[64,16,128]{2,1,0:T(8,128)(2,1)S(1)}, u32[]{:S(2)}, u32[]{:S(2)}) collective-permute-start(bf16[64,16,128]{2,1,0:T(8,128)(2,1)S(1)} %get-tuple-element.239), channel_id=1, source_target_pairs={{0,120},{8,0},{16,8},{24,16},{32,24},{40,32},{48,40},{56,48},{64,5... | collective-permute-start | bytes 786440 | tf_op jit(solution)/shard_map/while/body/eval_jaxpr/ppermute | solution.py:18
  606.9 8.0 %collective-permute-start = (bf16[64,16,128]{2,1,0:T(8,128)(2,1)S(1)}, bf16[64,16,128]{2,1,0:T(8,128)(2,1)S(1)}, u32[]{:S(2)}, u32[]{:S(2)}) collective-permute-start(bf16[64,16,128]{2,1,0:T(8,128)(2,1)S(1)} %get-tuple-element.239), channel_id=1, source_target_pairs={{0,120},{8,0},{16,8},{24,16},{32,24},{40,32},{48,40},{56,48},{64,5... | collective-permute-start | bytes 786440 | tf_op jit(solution)/shard_map/while/body/eval_jaxpr/ppermute | solution.py:18
  619.7 8.0 %collective-permute-start = (bf16[64,16,128]{2,1,0:T(8,128)(2,1)S(1)}, bf16[64,16,128]{2,1,0:T(8,128)(2,1)S(1)}, u32[]{:S(2)}, u32[]{:S(2)}) collective-permute-start(bf16[64,16,128]{2,1,0:T(8,128)(2,1)S(1)} %get-tuple-element.239), channel_id=1, source_target_pairs={{0,120},{8,0},{16,8},{24,16},{32,24},{40,32},{48,40},{56,48},{64,5... | collective-permute-start | bytes 786440 | tf_op jit(solution)/shard_map/while/body/eval_jaxpr/ppermute | solution.py:18
  632.6 8.0 %collective-permute-start = (bf16[64,16,128]{2,1,0:T(8,128)(2,1)S(1)}, bf16[64,16,128]{2,1,0:T(8,128)(2,1)S(1)}, u32[]{:S(2)}, u32[]{:S(2)}) collective-permute-start(bf16[64,16,128]{2,1,0:T(8,128)(2,1)S(1)} %get-tuple-element.239), channel_id=1, source_target_pairs={{0,120},{8,0},{16,8},{24,16},{32,24},{40,32},{48,40},{56,48},{64,5... | collective-permute-start | bytes 786440 | tf_op jit(solution)/shard_map/while/body/eval_jaxpr/ppermute | solution.py:18
  645.4 8.0 %collective-permute-start = (bf16[64,16,128]{2,1,0:T(8,128)(2,1)S(1)}, bf16[64,16,128]{2,1,0:T(8,128)(2,1)S(1)}, u32[]{:S(2)}, u32[]{:S(2)}) collective-permute-start(bf16[64,16,128]{2,1,0:T(8,128)(2,1)S(1)} %get-tuple-element.239), channel_id=1, source_target_pairs={{0,120},{8,0},{16,8},{24,16},{32,24},{40,32},{48,40},{56,48},{64,5... | collective-permute-start | bytes 786440 | tf_op jit(solution)/shard_map/while/body/eval_jaxpr/ppermute | solution.py:18
  658.2 8.0 %collective-permute-start = (bf16[64,16,128]{2,1,0:T(8,128)(2,1)S(1)}, bf16[64,16,128]{2,1,0:T(8,128)(2,1)S(1)}, u32[]{:S(2)}, u32[]{:S(2)}) collective-permute-start(bf16[64,16,128]{2,1,0:T(8,128)(2,1)S(1)} %get-tuple-element.239), channel_id=1, source_target_pairs={{0,120},{8,0},{16,8},{24,16},{32,24},{40,32},{48,40},{56,48},{64,5... | collective-permute-start | bytes 786440 | tf_op jit(solution)/shard_map/while/body/eval_jaxpr/ppermute | solution.py:18
where the time goes:
time: 695 us; the launch traced here: 686 us
  matrix products  293 us (42%)
  other arithmetic  209 us (30%)
  local copies, waits for them, and re-layouts  106 us (15%)
  waiting for transfers between devices  67.1 us (10%)
  starting transfers between devices  9.47 us (1%)
    add x16, other arithmetic, tap_step(): return frame + coeffs * piece.astype(jnp.float32)  173 us
    dynamic_slice x16, local copies, waits for them, and re-layouts, tap_step(): piece = lax.dynamic_slice_in_dim(segments, offset, SPECTRA, 2)  73.2 us
    dot_general x1, matrix products, per_device(): jnp.einsum(form_two, rotated_real, select_sin, preferred_element_type=jnp...  71.1 us
    dot_general x1, matrix products, per_device(): jnp.einsum(form_two, rotated_imag, select_sin, preferred_element_type=jnp...  64.2 us
    dot_general x1, matrix products, per_device(): jnp.einsum(form_two, rotated_imag, select_cos, preferred_element_type=jnp...  63.4 us
    dot_general x1, matrix products, per_device(): jnp.einsum(form_two, rotated_real, select_cos, preferred_element_type=jnp...  63.2 us
    ppermute x8, waiting for transfers between devices, shifted(): lax.ppermute(array, axis, [(i, (i + by) % length) for i in range(length)])  60.9 us
    dynamic_update_slice x8, other arithmetic, per_device(): moving, further = lax.scan(advance, local_block, None, length=distances - 1)  15.6 us
  transfers between devices with their start and end apart: 9, of which 9 were waited for; matrix products, arithmetic and copies ran while one was open for 0% of the time, Pallas kernels for 0%

commit v1 on v0

v1 whole, which is shorter than its diff:
```python
import functools
import math

import jax
import jax.numpy as jnp
import numpy as np
from jax import lax
from jax.experimental import pallas as pl
from jax.experimental.pallas import tpu as pltpu
from jax.sharding import PartitionSpec as P

NCH = 8192
FIRST = 64
SECOND = 128
TAPS = 16
SPECTRA = 16
SUBW = 4
CAP = 16
SEGMENTS = SPECTRA + TAPS - 1
LOCAL = 8
LANES = SPECTRA * 2 * SUBW
CHUNK = 1024
VMEM = 48 * 1024 * 1024


def table(length, rows, cols):
    angles = (np.outer(np.arange(rows), np.arange(cols)) % length) * (2.0 * math.pi / length)
    return np.cos(angles), np.sin(angles)


def complex_block(cosine, sine):
    return np.block([[cosine, -sine], [sine, cosine]])


def channelize_kernel(*refs):
    volts = refs[:SEGMENTS]
    taps, first_w, twid, second_w, lists, scale, out, frames, picked, turned = refs[SEGMENTS:]
    step = pl.program_id(0)
    per_step = CHUNK // SECOND

    def filter_one(at, carry):
        lanes = pl.ds(pl.multiple_of(at * SECOND, SECOND), SECOND)
        row = step * per_step + at
        coeffs = [jnp.broadcast_to(taps[j : j + 1, lanes], (LOCAL, SECOND)) for j in range(TAPS)]
        for part in range(2):
            sums = {}
            for seg in range(SEGMENTS):
                value = volts[seg][part, :, lanes].astype(jnp.float32)
                for j in range(TAPS):
                    t = seg - j
                    if 0 <= t < SPECTRA:
                        term = coeffs[j] * value
                        sums[t] = sums[t] + term if t in sums else term
                if seg >= TAPS - 1:
                    t = seg - TAPS + 1
                    frames[part, t, pl.ds(row, LOCAL, stride=FIRST), :] = sums.pop(t)
        return carry

    lax.fori_loop(0, per_step, filter_one, 0)

    @pl.when(step == pl.num_programs(0) - 1)
    def transform():
        number_m = lists[0:1, :]
        number_k = lists[1:2, :]
        onehot = (lax.broadcasted_iota(jnp.int32, (SECOND, 128), 0) == number_m).astype(jnp.bfloat16)
        chosen = jnp.concatenate(
            [
                jnp.dot(second_w[:, q * SECOND : (q + 1) * SECOND], onehot, preferred_element_type=jnp.float32)
                for q in range(2)
            ],
            axis=1,
        ).astype(jnp.bfloat16)
        half = lax.broadcasted_iota(jnp.int32, (8, 128), 0) // SUBW
        masks = [number_k == 2 * v + half for v in range(FIRST // 8)]
        low = half == 0
        group = 4

        def one(index, carry):
            i = index // (SPECTRA // group)
            t0 = (index % (SPECTRA // group)) * group
            rows = pl.ds(pl.multiple_of(i * FIRST, FIRST), FIRST)
            block = jnp.concatenate(
                [
                    jnp.concatenate([frames[part, t0 + n, rows, :] for part in range(2)], axis=0)
                    for n in range(group)
                ],
                axis=1,
            ).astype(jnp.bfloat16)
            first = jnp.dot(first_w[...], block, preferred_element_type=jnp.float32)
            rotated = []
            for n in range(group):
                real = first[:FIRST, n * SECOND : (n + 1) * SECOND]
                imag = first[FIRST:, n * SECOND : (n + 1) * SECOND]
                cosine, sine = twid[0], twid[1]
                rotated.append(
                    jnp.concatenate([real * cosine + imag * sine, imag * cosine - real * sine], axis=1)
                )
            rotated = jnp.concatenate(rotated, axis=0).astype(jnp.bfloat16)
            second = jnp.dot(rotated, chosen, preferred_element_type=jnp.float32)
            for n in range(group):
                folded = []
                for q in range(2):
                    total = jnp.zeros((8, 128), jnp.float32)
                    for v in range(FIRST // 8):
                        piece = second[n * FIRST + v * 8 : n * FIRST + v * 8 + 8, q * 128 : q * 128 + 128]
                        total = jnp.where(masks[v], piece, total)
                    folded.append(total + pltpu.roll(total, SUBW, 0))
                picked[i, pl.ds(pl.multiple_of((t0 + n) * 8, 8), 8), :] = jnp.where(low, folded[0], folded[1])
            return carry

        lax.fori_loop(0, LOCAL * SPECTRA // group, one, 0)
        for i in range(LOCAL):
            turned[pl.ds(i, 128, stride=LOCAL), :] = picked[i].T * scale[i]
        values = turned[...].reshape(8, CAP, LOCAL, LANES).astype(jnp.bfloat16)
        out[0] = values
        out[1] = values


def channelize(voltages, filter_taps, station_flags, subband_lists):
    cos1, sin1 = table(FIRST, FIRST, FIRST)
    cos2, sin2 = table(SECOND, SECOND, SECOND)
    first_w = jnp.asarray(complex_block(cos1, sin1).T, jnp.bfloat16)
    second_w = jnp.asarray(complex_block(cos2, sin2), jnp.bfloat16)
    twid = jnp.asarray(np.stack(table(NCH, FIRST, SECOND)), jnp.float32)
    flat = subband_lists.reshape(-1)
    lists = jnp.stack([flat // (FIRST // SUBW), flat % (FIRST // SUBW)])
    scale = jnp.repeat(station_flags, 2).astype(jnp.float32) / math.sqrt(NCH)
    steps = NCH // CHUNK

    def whole(*shape):
        return pl.BlockSpec(shape, lambda n: (0,) * len(shape))

    def segment(seg):
        return pl.BlockSpec((2, LOCAL, CHUNK), lambda n: (0, 0, seg * steps + n))

    return pl.pallas_call(
        channelize_kernel,
        grid=(steps,),
        in_specs=[segment(seg) for seg in range(SEGMENTS)]
        + [
            pl.BlockSpec((TAPS, CHUNK), lambda n: (0, n)),
            whole(2 * FIRST, 2 * FIRST),
            whole(2, FIRST, SECOND),
            whole(2 * SECOND, 2 * SECOND),
            whole(2, 128),
            pl.BlockSpec(memory_space=pltpu.SMEM),
        ],
        out_specs=whole(2, 8, CAP, LOCAL, LANES),
        out_shape=jax.ShapeDtypeStruct((2, 8, CAP, LOCAL, LANES), jnp.bfloat16),
        scratch_shapes=[
            pltpu.VMEM((2, SPECTRA, LOCAL * FIRST, SECOND), jnp.float32),
            pltpu.VMEM((LOCAL, LANES, 128), jnp.float32),
            pltpu.VMEM((128 * LOCAL, LANES), jnp.float32),
        ],
        compiler_params=pltpu.CompilerParams(vmem_limit_bytes=VMEM),
        name="channelize",
    )(*([voltages] * SEGMENTS), filter_taps, first_w, twid, second_w, lists, scale)


BSLOTS = 4


def correlate_kernel(count, first_call, *refs):
    places, live, own = refs[:3]
    others = refs[3 : 3 + count]
    out, results, sems = refs[-3:]
    step = pl.program_id(0)
    steps = pl.num_programs(0)
    lane = lax.broadcasted_iota(jnp.int32, (64, LANES), 1)
    real_lane = lane // SUBW % 2 == 0
    buf = step % 2

    def copies(at, slot):
        rows = pl.ds(at * BSLOTS * SUBW, BSLOTS * SUBW)
        return [
            pltpu.make_async_copy(results.at[slot, n], out.at[places[n], rows], sems.at[slot, n])
            for n in range(count)
        ]

    @pl.when(step >= 2)
    def reuse():
        for copy in copies(step - 2, buf):
            copy.wait()

    for k in range(BSLOTS):
        factor = live[step * BSLOTS + k]
        mine = own[:, k].astype(jnp.float32).reshape(64, LANES) * factor
        crossed = jnp.where(real_lane, pltpu.roll(mine, LANES - SUBW, 1), -pltpu.roll(mine, SUBW, 1))
        left = jnp.concatenate(
            [
                jnp.concatenate(
                    [jnp.where(lane % SUBW == u, x, 0.0).astype(jnp.bfloat16) for x in (mine, crossed)], axis=1
                )
                for u in range(SUBW)
            ],
            axis=0,
        )
        zero = jnp.zeros((64, LANES), jnp.bfloat16)
        for at in range(0, count, 2):
            right = []
            for n in range(at, min(at + 2, count)):
                block = others[n][:, k].reshape(64, LANES)
                right += [jnp.concatenate([block, zero], axis=1), jnp.concatenate([zero, block], axis=1)]
            right = jnp.concatenate(right, axis=0)
            product = lax.dot_general(
                left, right, (((1,), (1,)), ((), ())), preferred_element_type=jnp.float32
            )
            for n in range(at, min(at + 2, count)):
                piece = product[:, (n - at) * 128 : (n - at + 1) * 128]
                results[buf, n, k * SUBW : (k + 1) * SUBW] = piece.reshape(SUBW, 64, 128)

    for copy in copies(step, buf):
        copy.start()

    @pl.when(step == steps - 1)
    def finish():
        for copy in copies(step - 1, 1 - buf) + copies(step, buf):
            copy.wait()


def correlate(total, places, live, own, others):
    count = len(others)
    block = pl.BlockSpec((8, BSLOTS, LOCAL, LANES), lambda n: (0, n, 0, 0))
    shape = jax.ShapeDtypeStruct((9, CAP * SUBW, 64, 128), jnp.float32)
    args = [places, live, own, *others]
    specs = [pl.BlockSpec(memory_space=pltpu.SMEM)] * 2 + [block] * (1 + count)
    aliases = {}
    if total is not None:
        aliases = {len(args): 0}
        args.append(total)
        specs.append(pl.BlockSpec(memory_space=pl.ANY))
    return pl.pallas_call(
        functools.partial(correlate_kernel, count, total is None),
        grid=(CAP // BSLOTS,),
        in_specs=specs,
        out_specs=pl.BlockSpec(memory_space=pl.ANY),
        out_shape=shape,
        scratch_shapes=[
            pltpu.VMEM((2, count, BSLOTS * SUBW, 64, 128), jnp.float32),
            pltpu.SemaphoreType.DMA((2, count)),
        ],
        input_output_aliases=aliases,
        compiler_params=pltpu.CompilerParams(vmem_limit_bytes=VMEM),
        name="correlate",
    )(*args)


def per_device(voltages, filter_taps, station_flags, subband_lists, subband_counts):
    stn = lax.axis_index("stn")
    row, col, core = stn // 8, stn // 2 % 4, stn % 2
    group = lax.axis_index("chan")
    count = lax.dynamic_index_in_dim(subband_counts, group, 0, keepdims=False)
    live = (jnp.arange(CAP, dtype=jnp.int32) < count).astype(jnp.float32) / SPECTRA

    selected = channelize(voltages, filter_taps, station_flags, subband_lists)
    selected = selected.reshape(16, CAP, LOCAL, LANES)
    members = [
        [(y * 8 + z * 2 + c) * 8 + g for y in range(2) for g in range(8)] for z in range(4) for c in range(2)
    ]
    rows = lax.all_to_all(selected, ("stn", "chan"), 0, 0, axis_index_groups=members, tiled=True)
    rows = rows.reshape(2, 8, CAP, LOCAL, LANES)

    def take(r):
        return lax.dynamic_index_in_dim(rows, r, 0, keepdims=False)

    def exchange(array, flip):
        return lax.ppermute(array, "stn", [(i, i ^ flip) for i in range(16)])

    own = take(row)
    far = take(1 - row)
    moved = {}
    for flip in (2, 1, 3):
        other = col ^ flip
        moved[flip] = exchange(jnp.where(col > other, own, far), flip * 2)
    spare = exchange(jnp.where(core == 0, far, own), 1)
    passed = {flip: exchange(moved[flip], 1) for flip in (1, 3, 2)}

    side = 1 - 2 * core
    ahead = {flip: 2 * ((col ^ flip) - col + 4) % 8 for flip in (1, 2, 3)}
    total = correlate(
        None, jnp.stack([0 * core, 8 + 0 * core, 1 + 6 * core]).astype(jnp.int32), live, own, [own, far, spare]
    )
    total = correlate(
        total,
        jnp.stack([ahead[1], ahead[3], ahead[1] + side, ahead[3] + side]).astype(jnp.int32),
        live,
        own,
        [moved[1], moved[3], passed[1], passed[3]],
    )
    total = correlate(
        total, jnp.stack([ahead[2], ahead[2] + side]).astype(jnp.int32), live, own, [moved[2], passed[2]]
    )
    return total[None]


def solution(mesh):
    placed = (P(None, ("stn", "chan"), None), P(), P(("stn", "chan")), P(), P())
    return jax.shard_map(
        per_device,
        mesh=mesh,
        in_specs=placed,
        out_specs=P("stn", None, "chan", None, None),
        check_vma=False,
    )
```

time: 695 us -> 84.1 us (0.12)
  the two profiles are of different devices: /device:TPU:97 before, /device:TPU:1 now
where the time goes in v1:
time: 84.1 us; the launch traced here: 83.6 us
  Pallas kernels  42.5 us (51%)
  starting transfers between devices  22.2 us (26%)
  waiting for transfers between devices  12.2 us (15%)
  local copies, waits for them, and re-layouts  5.01 us (6%)
  other arithmetic  1.57 us (2%)
    pallas_call x1, Pallas kernels, channelize(): pl.pallas_call(channelize_kernel, grid=(steps,), in_specs=[segment(seg) f...  29.5 us
    ppermute x7, starting transfers between devices, exchange(): return lax.ppermute(array, 'stn', [(i, i ^ flip) for i in range(16)])  14.6 us
    pallas_call x3, Pallas kernels, correlate(): pl.pallas_call(functools.partial(correlate_kernel, count, total is None),...  13.1 us
    all_to_all x1, waiting for transfers between devices, per_device(): lax.all_to_all(selected, ('stn', 'chan'), 0, 0, axis_index_groups=members...  9.94 us
    all_to_all x1, starting transfers between devices, per_device(): lax.all_to_all(selected, ('stn', 'chan'), 0, 0, axis_index_groups=members...  7.6 us
    unnamed x10, local copies, waits for them, and re-layouts  3.54 us
    ppermute x7, waiting for transfers between devices, exchange(): return lax.ppermute(array, 'stn', [(i, i ^ flip) for i in range(16)])  2.22 us
  transfers between devices with their start and end apart: 8, of which 2 were waited for; matrix products, arithmetic and copies ran while one was open for 2% of the time, Pallas kernels for 11%

profile of v1, /device:TPU:1, one launch (start us, length us, event | category | flops | bytes accessed | tf_op | source)
XLA Modules:
  0.0 83.6 jit_solution(18204072073977024168)
XLA Ops:
  0.0 0.8 reshape.115
  0.8 0.7 convert_multiply_fusion
  1.5 0.1 div.44.refs_36_
  1.6 1.0 %copy-done = f32[16,8192]{1,0:T(8,128)S(1)} copy-done((f32[16,8192]{1,0:T(8,128)S(1)}, f32[16,8192]{1,0:T(8,128)}, u32[]{:S(2)}) %copy-start) | copy-done | bytes 524312
  2.7 0.9 %copy-done.1 = bf16[256,256]{1,0:T(8,128)(2,1)S(1)} copy-done((bf16[256,256]{1,0:T(8,128)(2,1)S(1)}, bf16[256,256]{1,0:T(8,128)(2,1)}, u32[]{:S(2)}) %copy-start.1) | copy-done | bytes 131096
  3.6 0.8 %copy-done.2 = f32[2,64,128]{2,1,0:T(8,128)S(1)} copy-done((f32[2,64,128]{2,1,0:T(8,128)S(1)}, f32[2,64,128]{2,1,0:T(8,128)}, u32[]{:S(2)}) %copy-start.2) | copy-done | bytes 65560
  4.4 0.8 copy-done.3
  5.2 29.5 %channelize.1 = bf16[2,8,16,8,128]{4,3,2,1,0:T(8,128)(2,1)} custom-call(bf16[2,8,253952]{2,1,0:T(8,128)(2,1)} %refs_30_.1, bf16[2,8,253952]{2,1,0:T(8,128)(2,1)} %refs_30_.1, bf16[2,8,253952]{2,1,0:T(8,128)(2,1)} %refs_30_.1, bf16[2,8,253952]{2,1,0:T(8,128)(2,1)} %refs_30_.1, bf16[2,8,253952]{2,1,0:T(8,128)(2,1)} %refs_30_.1, ...), custom_call_target="tpu_custom_call" | custom-call | tf_op jit(solution)/shard_map/channelize/pallas_call | solution.py:136
  34.6 7.6 %all-to-all-start = ((bf16[16,16,8,128]{3,2,1,0:T(8,128)(2,1)}), bf16[16,16,8,128]{3,2,1,0:T(8,128)(2,1)S(1)}, u32[]{:S(2)}, u32[]{:S(2)}) async-start(bf16[16,16,8,128]{3,2,1,0:T(8,128)(2,1)} %bitcast.3), calls=%async_computation | async-start | bytes 1048576 | tf_op jit(solution)/shard_map/all_to_all | solution.py:260
  42.3 9.9 %all-to-all-done = bf16[16,16,8,128]{3,2,1,0:T(8,128)(2,1)S(1)} async-done(((bf16[16,16,8,128]{3,2,1,0:T(8,128)(2,1)}), bf16[16,16,8,128]{3,2,1,0:T(8,128)(2,1)S(1)}, u32[]{:S(2)}, u32[]{:S(2)}) %all-to-all-start) | async-done | bytes 524320 | tf_op jit(solution)/shard_map/all_to_all | solution.py:260
  52.3 1.7 %collective-permute-start.2 = (bf16[8,16,8,128]{3,2,1,0:T(8,128)(2,1)S(1)}, bf16[8,16,8,128]{3,2,1,0:T(8,128)(2,1)S(1)}, u32[]{:S(2)}, u32[]{:S(2)}) collective-permute-start(bf16[8,16,8,128]{3,2,1,0:T(8,128)(2,1)S(1)} %get-tuple-element.9), channel_id=1, source_target_pairs={{0,16},{8,24},{16,0},{24,8},{32,48},{40,56},{48,32},{56,40},{64,80... | collective-permute-start | bytes 786440 | tf_op jit(solution)/shard_map/ppermute | solution.py:267
  54.1 2.3 %collective-permute-start.3 = (bf16[8,16,8,128]{3,2,1,0:T(8,128)(2,1)S(1)}, bf16[8,16,8,128]{3,2,1,0:T(8,128)(2,1)S(1)}, u32[]{:S(2)}, u32[]{:S(2)}) collective-permute-start(bf16[8,16,8,128]{3,2,1,0:T(8,128)(2,1)S(1)} %get-tuple-element.8), channel_id=1, source_target_pairs={{0,48},{8,56},{16,32},{24,40},{32,16},{40,24},{48,0},{56,8},{64,11... | collective-permute-start | bytes 786440 | tf_op jit(solution)/shard_map/ppermute | solution.py:267
  56.3 1.1 %collective-permute-start = (bf16[8,16,8,128]{3,2,1,0:T(8,128)(2,1)S(1)}, bf16[8,16,8,128]{3,2,1,0:T(8,128)(2,1)S(1)}, u32[]{:S(2)}, u32[]{:S(2)}) collective-permute-start(bf16[8,16,8,128]{3,2,1,0:T(8,128)(2,1)S(1)} %get-tuple-element.10), channel_id=1, source_target_pairs={{0,32},{8,40},{16,48},{24,56},{32,0},{40,8},{48,16},{56,24},{64,96... | collective-permute-start | bytes 786440 | tf_op jit(solution)/shard_map/ppermute | solution.py:267
  57.4 0.6 dynamic_slice.11
  57.9 0.5 compare_select_fusion.refs_1_
  58.5 3.0 %collective-permute-start.6 = (bf16[8,16,8,128]{3,2,1,0:T(8,128)(2,1)S(1)}, bf16[8,16,8,128]{3,2,1,0:T(8,128)(2,1)S(1)}, u32[]{:S(2)}, u32[]{:S(2)}) collective-permute-start(bf16[8,16,8,128]{3,2,1,0:T(8,128)(2,1)S(1)} %get-tuple-element.5), channel_id=1, source_target_pairs={{0,8},{8,0},{16,24},{24,16},{32,40},{40,32},{48,56},{56,48},{64,72... | collective-permute-start | bytes 786440 | tf_op jit(solution)/shard_map/ppermute | solution.py:267
  61.5 2.2 %collective-permute-start.4 = (bf16[8,16,8,128]{3,2,1,0:T(8,128)(2,1)S(1)}, bf16[8,16,8,128]{3,2,1,0:T(8,128)(2,1)S(1)}, u32[]{:S(2)}, u32[]{:S(2)}) collective-permute-start(bf16[8,16,8,128]{3,2,1,0:T(8,128)(2,1)S(1)} %collective-permute-done.2.refs_3_), channel_id=1, source_target_pairs={{0,8},{8,0},{16,24},{24,16},{32,40},{40,32},{48,56},{56,48},{64,72... | collective-permute-start | bytes 786440 | tf_op jit(solution)/shard_map/ppermute | solution.py:267
  63.7 2.2 %collective-permute-done.3.refs_4_ = bf16[8,16,8,128]{3,2,1,0:T(8,128)(2,1)S(1)} collective-permute-done((bf16[8,16,8,128]{3,2,1,0:T(8,128)(2,1)S(1)}, bf16[8,16,8,128]{3,2,1,0:T(8,128)(2,1)S(1)}, u32[]{:S(2)}, u32[]{:S(2)}) %collective-permute-start.3) | collective-permute-done | bytes 262176 | tf_op jit(solution)/shard_map/ppermute | solution.py:267
  66.0 2.5 %collective-permute-start.5 = (bf16[8,16,8,128]{3,2,1,0:T(8,128)(2,1)S(1)}, bf16[8,16,8,128]{3,2,1,0:T(8,128)(2,1)S(1)}, u32[]{:S(2)}, u32[]{:S(2)}) collective-permute-start(bf16[8,16,8,128]{3,2,1,0:T(8,128)(2,1)S(1)} %collective-permute-done.3.refs_4_), channel_id=1, source_target_pairs={{0,8},{8,0},{16,24},{24,16},{32,40},{40,32},{48,56},{56,48},{64,72... | collective-permute-start | bytes 786440 | tf_op jit(solution)/shard_map/ppermute | solution.py:267
  68.5 1.8 %collective-permute-start.1 = (bf16[8,16,8,128]{3,2,1,0:T(8,128)(2,1)S(1)}, bf16[8,16,8,128]{3,2,1,0:T(8,128)(2,1)S(1)}, u32[]{:S(2)}, u32[]{:S(2)}) collective-permute-start(bf16[8,16,8,128]{3,2,1,0:T(8,128)(2,1)S(1)} %collective-permute-done.refs_3_), channel_id=1, source_target_pairs={{0,8},{8,0},{16,24},{24,16},{32,40},{40,32},{48,56},{56,48},{64,72... | collective-permute-start | bytes 786440 | tf_op jit(solution)/shard_map/ppermute | solution.py:267
  70.4 0.1 pad_add_fusion.2.refs_0_
  70.5 4.4 %correlate.3.refs_7_ = f32[9,64,64,128]{3,2,1,0:T(8,128)} custom-call(s32[3]{0:T(128)S(1)} %pad_add_fusion.3.refs_0_, f32[16]{0:T(128)S(1)} %compare_select_fusion.refs_1_, bf16[8,16,8,128]{3,2,1,0:T(8,128)(2,1)S(1)} %get-tuple-element.7.refs_2_.refs_3_, bf16[8,16,8,128]{3,2,1,0:T(8,128)(2,1)S(1)} %get-tuple-element.7.refs_2_.refs_3_, ...), custom_call_target="tpu_custom_call" | custom-call | tf_op jit(solution)/shard_map/correlate/pallas_call | solution.py:232
  74.9 4.9 %correlate.4.refs_5_ = f32[9,64,64,128]{3,2,1,0:T(8,128)} custom-call(s32[4]{0:T(128)S(1)} %pad_add_fusion.2.refs_0_, f32[16]{0:T(128)S(1)} %compare_select_fusion.refs_1_, bf16[8,16,8,128]{3,2,1,0:T(8,128)(2,1)S(1)} %get-tuple-element.7.refs_2_.refs_3_, bf16[8,16,8,128]{3,2,1,0:T(8,128)(2,1)S(1)} %collective-permute-done.2.refs_3_, ...), custom_call_target="tpu_custom_call", output_to_operand_aliasing={{}: (7, {})} | custom-call | tf_op jit(solution)/shard_map/correlate/pallas_call | solution.py:232
  79.9 3.7 %correlate.5 = f32[9,64,64,128]{3,2,1,0:T(8,128)} custom-call(s32[2]{0:T(128)S(1)} %pad_add_fusion.1.refs_0_, f32[16]{0:T(128)S(1)} %compare_select_fusion.refs_1_, bf16[8,16,8,128]{3,2,1,0:T(8,128)(2,1)S(1)} %get-tuple-element.7.refs_2_.refs_3_, bf16[8,16,8,128]{3,2,1,0:T(8,128)(2,1)S(1)} %collective-permute-done.refs_3_, ...), custom_call_target="tpu_custom_call", output_to_operand_aliasing={{}: (5, {})} | custom-call | tf_op jit(solution)/shard_map/correlate/pallas_call | solution.py:232
  (19 shorter events, 0.4 us)
Async XLA Ops:
  1.6 1.0 %copy-start = (f32[16,8192]{1,0:T(8,128)S(1)}, f32[16,8192]{1,0:T(8,128)}, u32[]{:S(2)}) copy-start(f32[16,8192]{1,0:T(8,128)} %refs_31_.1) | copy-start | bytes 1572868
  2.7 0.9 %copy-start.1 = (bf16[256,256]{1,0:T(8,128)(2,1)S(1)}, bf16[256,256]{1,0:T(8,128)(2,1)}, u32[]{:S(2)}) copy-start(bf16[256,256]{1,0:T(8,128)(2,1)} %constant.128.clone.refs_34_) | copy-start | bytes 393220
  3.6 0.8 %copy-start.2 = (f32[2,64,128]{2,1,0:T(8,128)S(1)}, f32[2,64,128]{2,1,0:T(8,128)}, u32[]{:S(2)}) copy-start(f32[2,64,128]{2,1,0:T(8,128)} %constant.129.clone.refs_33_) | copy-start | bytes 196612
  4.4 0.8 copy-start.3
  5.2 52.2 %copy-start.4 = (s32[8]{0:T(128)S(1)}, s32[8]{0:T(128)}, u32[]{:S(2)}) copy-start(s32[8]{0:T(128)} %param.12) | copy-start | bytes 100
  34.6 17.6 %all-to-all-start = ((bf16[16,16,8,128]{3,2,1,0:T(8,128)(2,1)}), bf16[16,16,8,128]{3,2,1,0:T(8,128)(2,1)S(1)}, u32[]{:S(2)}, u32[]{:S(2)}) async-start(bf16[16,16,8,128]{3,2,1,0:T(8,128)(2,1)} %bitcast.3), calls=%async_computation | async-start | bytes 1048576 | tf_op jit(solution)/shard_map/all_to_all | solution.py:260
  52.3 9.2 %collective-permute-start.2 = (bf16[8,16,8,128]{3,2,1,0:T(8,128)(2,1)S(1)}, bf16[8,16,8,128]{3,2,1,0:T(8,128)(2,1)S(1)}, u32[]{:S(2)}, u32[]{:S(2)}) collective-permute-start(bf16[8,16,8,128]{3,2,1,0:T(8,128)(2,1)S(1)} %get-tuple-element.9), channel_id=1, source_target_pairs={{0,16},{8,24},{16,0},{24,8},{32,48},{40,56},{48,32},{56,40},{64,80... | collective-permute-start | bytes 786440 | tf_op jit(solution)/shard_map/ppermute | solution.py:267
  54.1 11.9 %collective-permute-start.3 = (bf16[8,16,8,128]{3,2,1,0:T(8,128)(2,1)S(1)}, bf16[8,16,8,128]{3,2,1,0:T(8,128)(2,1)S(1)}, u32[]{:S(2)}, u32[]{:S(2)}) collective-permute-start(bf16[8,16,8,128]{3,2,1,0:T(8,128)(2,1)S(1)} %get-tuple-element.8), channel_id=1, source_target_pairs={{0,48},{8,56},{16,32},{24,40},{32,16},{40,24},{48,0},{56,8},{64,11... | collective-permute-start | bytes 786440 | tf_op jit(solution)/shard_map/ppermute | solution.py:267
  56.3 12.1 %collective-permute-start = (bf16[8,16,8,128]{3,2,1,0:T(8,128)(2,1)S(1)}, bf16[8,16,8,128]{3,2,1,0:T(8,128)(2,1)S(1)}, u32[]{:S(2)}, u32[]{:S(2)}) collective-permute-start(bf16[8,16,8,128]{3,2,1,0:T(8,128)(2,1)S(1)} %get-tuple-element.10), channel_id=1, source_target_pairs={{0,32},{8,40},{16,48},{24,56},{32,0},{40,8},{48,16},{56,24},{64,96... | collective-permute-start | bytes 786440 | tf_op jit(solution)/shard_map/ppermute | solution.py:267
  58.5 12.0 %collective-permute-start.6 = (bf16[8,16,8,128]{3,2,1,0:T(8,128)(2,1)S(1)}, bf16[8,16,8,128]{3,2,1,0:T(8,128)(2,1)S(1)}, u32[]{:S(2)}, u32[]{:S(2)}) collective-permute-start(bf16[8,16,8,128]{3,2,1,0:T(8,128)(2,1)S(1)} %get-tuple-element.5), channel_id=1, source_target_pairs={{0,8},{8,0},{16,24},{24,16},{32,40},{40,32},{48,56},{56,48},{64,72... | collective-permute-start | bytes 786440 | tf_op jit(solution)/shard_map/ppermute | solution.py:267
  61.5 13.4 %collective-permute-start.4 = (bf16[8,16,8,128]{3,2,1,0:T(8,128)(2,1)S(1)}, bf16[8,16,8,128]{3,2,1,0:T(8,128)(2,1)S(1)}, u32[]{:S(2)}, u32[]{:S(2)}) collective-permute-start(bf16[8,16,8,128]{3,2,1,0:T(8,128)(2,1)S(1)} %collective-permute-done.2.refs_3_), channel_id=1, source_target_pairs={{0,8},{8,0},{16,24},{24,16},{32,40},{40,32},{48,56},{56,48},{64,72... | collective-permute-start | bytes 786440 | tf_op jit(solution)/shard_map/ppermute | solution.py:267
  66.0 9.0 %collective-permute-start.5 = (bf16[8,16,8,128]{3,2,1,0:T(8,128)(2,1)S(1)}, bf16[8,16,8,128]{3,2,1,0:T(8,128)(2,1)S(1)}, u32[]{:S(2)}, u32[]{:S(2)}) collective-permute-start(bf16[8,16,8,128]{3,2,1,0:T(8,128)(2,1)S(1)} %collective-permute-done.3.refs_4_), channel_id=1, source_target_pairs={{0,8},{8,0},{16,24},{24,16},{32,40},{40,32},{48,56},{56,48},{64,72... | collective-permute-start | bytes 786440 | tf_op jit(solution)/shard_map/ppermute | solution.py:267
  68.5 11.4 %collective-permute-start.1 = (bf16[8,16,8,128]{3,2,1,0:T(8,128)(2,1)S(1)}, bf16[8,16,8,128]{3,2,1,0:T(8,128)(2,1)S(1)}, u32[]{:S(2)}, u32[]{:S(2)}) collective-permute-start(bf16[8,16,8,128]{3,2,1,0:T(8,128)(2,1)S(1)} %collective-permute-done.refs_3_), channel_id=1, source_target_pairs={{0,8},{8,0},{16,24},{24,16},{32,40},{40,32},{48,56},{56,48},{64,72... | collective-permute-start | bytes 786440 | tf_op jit(solution)/shard_map/ppermute | solution.py:267

commit v2 on v1

--- a/solution.py
+++ b/solution.py
@@ -20,7 +20,11 @@
 LOCAL = 8
 LANES = SPECTRA * 2 * SUBW
 CHUNK = 1024
+PITCH = FIRST + 8
+GROUP = 8
+UNROLL = 8
 VMEM = 48 * 1024 * 1024
+VMEM_ALL = 60 * 1024 * 1024
 
 
 def table(length, rows, cols):
@@ -33,10 +37,22 @@
 
 
 def channelize_kernel(*refs):
-    volts = refs[:SEGMENTS]
-    taps, first_w, twid, second_w, lists, scale, out, frames, picked, turned = refs[SEGMENTS:]
+    volts, taps, first_hbm, twid_hbm, second_hbm, lists, flags, out = refs[:8]
+    frames, picked, turned, first_w, twid, second_w, sems = refs[8:]
     step = pl.program_id(0)
     per_step = CHUNK // SECOND
+
+    copies = [
+        pltpu.make_async_copy(source, target, sems.at[n])
+        for n, (source, target) in enumerate(
+            ((first_hbm, first_w), (twid_hbm, twid), (second_hbm, second_w))
+        )
+    ]
+
+    @pl.when(step == 0)
+    def fetch():
+        for copy in copies:
+            copy.start()
 
     def filter_one(at, carry):
         lanes = pl.ds(pl.multiple_of(at * SECOND, SECOND), SECOND)
@@ -45,7 +61,7 @@
         for part in range(2):
             sums = {}
             for seg in range(SEGMENTS):
-                value = volts[seg][part, :, lanes].astype(jnp.float32)
+                value = volts[part, seg, :, lanes].astype(jnp.float32)
                 for j in range(TAPS):
                     t = seg - j
                     if 0 <= t < SPECTRA:
@@ -53,15 +69,29 @@
                         sums[t] = sums[t] + term if t in sums else term
                 if seg >= TAPS - 1:
                     t = seg - TAPS + 1
-                    frames[part, t, pl.ds(row, LOCAL, stride=FIRST), :] = sums.pop(t)
+                    frames[part, t, pl.ds(row, LOCAL, stride=PITCH), :] = sums.pop(t)
         return carry
 
-    lax.fori_loop(0, per_step, filter_one, 0)
+    lax.fori_loop(0, per_step, filter_one, 0, unroll=2)
 
     @pl.when(step == pl.num_programs(0) - 1)
     def transform():
-        number_m = lists[0:1, :]
-        number_k = lists[1:2, :]
+        for copy in copies:
+            copy.wait()
+        spread = lax.broadcasted_iota(jnp.int32, (CAP, 128), 1) % CAP == lax.broadcasted_iota(
+            jnp.int32, (CAP, 128), 0
+        )
+        spread = spread.astype(jnp.bfloat16)
+        diagonal = lax.broadcasted_iota(jnp.int32, (8, 128), 1) // CAP == lax.broadcasted_iota(
+            jnp.int32, (8, 128), 0
+        )
+
+        def along_lanes(numbers):
+            full = jnp.dot(numbers.astype(jnp.bfloat16), spread, preferred_element_type=jnp.float32)
+            return jnp.sum(jnp.where(diagonal, full, 0.0), axis=0, keepdims=True).astype(jnp.int32)
+
+        number_m = along_lanes(lists[...] // (FIRST // SUBW))
+        number_k = along_lanes(lists[...] % (FIRST // SUBW))
         onehot = (lax.broadcasted_iota(jnp.int32, (SECOND, 128), 0) == number_m).astype(jnp.bfloat16)
         chosen = jnp.concatenate(
             [
@@ -73,12 +103,12 @@
         half = lax.broadcasted_iota(jnp.int32, (8, 128), 0) // SUBW
         masks = [number_k == 2 * v + half for v in range(FIRST // 8)]
         low = half == 0
-        group = 4
+        group = GROUP
 
         def one(index, carry):
             i = index // (SPECTRA // group)
             t0 = (index % (SPECTRA // group)) * group
-            rows = pl.ds(pl.multiple_of(i * FIRST, FIRST), FIRST)
+            rows = pl.ds(pl.multiple_of(i * PITCH, 8), FIRST)
             block = jnp.concatenate(
                 [
                     jnp.concatenate([frames[part, t0 + n, rows, :] for part in range(2)], axis=0)
@@ -108,9 +138,9 @@
                 picked[i, pl.ds(pl.multiple_of((t0 + n) * 8, 8), 8), :] = jnp.where(low, folded[0], folded[1])
             return carry
 
-        lax.fori_loop(0, LOCAL * SPECTRA // group, one, 0)
+        lax.fori_loop(0, LOCAL * SPECTRA // group, one, 0, unroll=UNROLL)
         for i in range(LOCAL):
-            turned[pl.ds(i, 128, stride=LOCAL), :] = picked[i].T * scale[i]
+            turned[pl.ds(i, 128, stride=LOCAL), :] = picked[i].T * (flags[i // 2].astype(jnp.float32) * (1.0 / math.sqrt(NCH)))
         values = turned[...].reshape(8, CAP, LOCAL, LANES).astype(jnp.bfloat16)
         out[0] = values
         out[1] = values
@@ -122,46 +152,46 @@
     first_w = jnp.asarray(complex_block(cos1, sin1).T, jnp.bfloat16)
     second_w = jnp.asarray(complex_block(cos2, sin2), jnp.bfloat16)
     twid = jnp.asarray(np.stack(table(NCH, FIRST, SECOND)), jnp.float32)
-    flat = subband_lists.reshape(-1)
-    lists = jnp.stack([flat // (FIRST // SUBW), flat % (FIRST // SUBW)])
-    scale = jnp.repeat(station_flags, 2).astype(jnp.float32) / math.sqrt(NCH)
     steps = NCH // CHUNK
+    volts = voltages.reshape(2, LOCAL, SEGMENTS, NCH).transpose(0, 2, 1, 3)
 
     def whole(*shape):
         return pl.BlockSpec(shape, lambda n: (0,) * len(shape))
 
-    def segment(seg):
-        return pl.BlockSpec((2, LOCAL, CHUNK), lambda n: (0, 0, seg * steps + n))
-
+    hbm = pl.BlockSpec(memory_space=pltpu.HBM)
     return pl.pallas_call(
         channelize_kernel,
         grid=(steps,),
-        in_specs=[segment(seg) for seg in range(SEGMENTS)]
-        + [
+        in_specs=[
+            pl.BlockSpec((2, SEGMENTS, LOCAL, CHUNK), lambda n: (0, 0, 0, n)),
             pl.BlockSpec((TAPS, CHUNK), lambda n: (0, n)),
-            whole(2 * FIRST, 2 * FIRST),
-            whole(2, FIRST, SECOND),
-            whole(2 * SECOND, 2 * SECOND),
-            whole(2, 128),
+            hbm,
+            hbm,
+            hbm,
+            whole(8, CAP),
             pl.BlockSpec(memory_space=pltpu.SMEM),
         ],
         out_specs=whole(2, 8, CAP, LOCAL, LANES),
         out_shape=jax.ShapeDtypeStruct((2, 8, CAP, LOCAL, LANES), jnp.bfloat16),
         scratch_shapes=[
-            pltpu.VMEM((2, SPECTRA, LOCAL * FIRST, SECOND), jnp.float32),
+            pltpu.VMEM((2, SPECTRA, LOCAL * PITCH, SECOND), jnp.float32),
             pltpu.VMEM((LOCAL, LANES, 128), jnp.float32),
             pltpu.VMEM((128 * LOCAL, LANES), jnp.float32),
+            pltpu.VMEM((2 * FIRST, 2 * FIRST), jnp.bfloat16),
+            pltpu.VMEM((2, FIRST, SECOND), jnp.float32),
+            pltpu.VMEM((2 * SECOND, 2 * SECOND), jnp.bfloat16),
+            pltpu.SemaphoreType.DMA((3,)),
         ],
-        compiler_params=pltpu.CompilerParams(vmem_limit_bytes=VMEM),
+        compiler_params=pltpu.CompilerParams(vmem_limit_bytes=VMEM_ALL),
         name="channelize",
-    )(*([voltages] * SEGMENTS), filter_taps, first_w, twid, second_w, lists, scale)
-
-
-BSLOTS = 4
-
-
-def correlate_kernel(count, first_call, *refs):
-    places, live, own = refs[:3]
+    )(volts, filter_taps, first_w, twid, second_w, subband_lists, station_flags)
+
+
+BSLOTS = 8
+
+
+def correlate_kernel(count, *refs):
+    places, counts, own = refs[:3]
     others = refs[3 : 3 + count]
     out, results, sems = refs[-3:]
     step = pl.program_id(0)
@@ -173,7 +203,7 @@
     def copies(at, slot):
         rows = pl.ds(at * BSLOTS * SUBW, BSLOTS * SUBW)
         return [
-            pltpu.make_async_copy(results.at[slot, n], out.at[places[n], rows], sems.at[slot, n])
+            pltpu.make_async_copy(results.at[slot, n], out.at[places[n + 1], rows], sems.at[slot, n])
             for n in range(count)
         ]
 
@@ -183,7 +213,7 @@
             copy.wait()
 
     for k in range(BSLOTS):
-        factor = live[step * BSLOTS + k]
+        factor = jnp.where(step * BSLOTS + k < counts[places[0]], 1.0 / SPECTRA, 0.0)
         mine = own[:, k].astype(jnp.float32).reshape(64, LANES) * factor
         crossed = jnp.where(real_lane, pltpu.roll(mine, LANES - SUBW, 1), -pltpu.roll(mine, SUBW, 1))
         left = jnp.concatenate(
@@ -218,11 +248,13 @@
             copy.wait()
 
 
-def correlate(total, places, live, own, others):
+def correlate(total, group, counts, own, pairs):
+    places = jnp.stack([group] + [distance for distance, _ in pairs]).astype(jnp.int32)
+    others = [block for _, block in pairs]
     count = len(others)
     block = pl.BlockSpec((8, BSLOTS, LOCAL, LANES), lambda n: (0, n, 0, 0))
     shape = jax.ShapeDtypeStruct((9, CAP * SUBW, 64, 128), jnp.float32)
-    args = [places, live, own, *others]
+    args = [places, counts, own, *others]
     specs = [pl.BlockSpec(memory_space=pltpu.SMEM)] * 2 + [block] * (1 + count)
     aliases = {}
     if total is not None:
@@ -230,7 +262,7 @@
         args.append(total)
         specs.append(pl.BlockSpec(memory_space=pl.ANY))
     return pl.pallas_call(
-        functools.partial(correlate_kernel, count, total is None),
+        functools.partial(correlate_kernel, count),
         grid=(CAP // BSLOTS,),
         in_specs=specs,
         out_specs=pl.BlockSpec(memory_space=pl.ANY),
@@ -249,8 +281,6 @@
     stn = lax.axis_index("stn")
     row, col, core = stn // 8, stn // 2 % 4, stn % 2
     group = lax.axis_index("chan")
-    count = lax.dynamic_index_in_dim(subband_counts, group, 0, keepdims=False)
-    live = (jnp.arange(CAP, dtype=jnp.int32) < count).astype(jnp.float32) / SPECTRA
 
     selected = channelize(voltages, filter_taps, station_flags, subband_lists)
     selected = selected.reshape(16, CAP, LOCAL, LANES)
@@ -273,23 +303,18 @@
         other = col ^ flip
         moved[flip] = exchange(jnp.where(col > other, own, far), flip * 2)
     spare = exchange(jnp.where(core == 0, far, own), 1)
-    passed = {flip: exchange(moved[flip], 1) for flip in (1, 3, 2)}
 
     side = 1 - 2 * core
     ahead = {flip: 2 * ((col ^ flip) - col + 4) % 8 for flip in (1, 2, 3)}
-    total = correlate(
-        None, jnp.stack([0 * core, 8 + 0 * core, 1 + 6 * core]).astype(jnp.int32), live, own, [own, far, spare]
-    )
-    total = correlate(
-        total,
-        jnp.stack([ahead[1], ahead[3], ahead[1] + side, ahead[3] + side]).astype(jnp.int32),
-        live,
-        own,
-        [moved[1], moved[3], passed[1], passed[3]],
-    )
-    total = correlate(
-        total, jnp.stack([ahead[2], ahead[2] + side]).astype(jnp.int32), live, own, [moved[2], passed[2]]
-    )
+    join = functools.partial(correlate, group=group, counts=subband_counts, own=own)
+    total = join(None, pairs=[(0 * core, own), (0 * core + 8, far), (1 + 6 * core, spare)])
+    for flips in ((1, 3), (2,)):
+        arrived = [moved[flip] for flip in flips]
+        *arrived, total = lax.optimization_barrier((*arrived, total))
+        pairs = []
+        for flip, block in zip(flips, arrived):
+            pairs += [(ahead[flip], block), (ahead[flip] + side, exchange(block, 1))]
+        total = join(total, pairs=pairs)
     return total[None]
 
 

time: 84.1 us -> 63 us (0.75)
  Pallas kernels: 42.5 us -> 27.3 us
  starting transfers between devices: 22.2 us -> 16.4 us
  waiting for transfers between devices: 12.2 us -> 17.8 us
  local copies, waits for them, and re-layouts: 5.01 us -> 0.75 us
  other arithmetic: 1.57 us -> 0.26 us
    pallas_call x4, Pallas kernels: 42.5 us -> 27.3 us  [the longest x1 15.3 us: channelize(): pl.pallas_call(channelize_kernel, grid=(steps,), in_specs=[pl.BlockSpec((...]
    ppermute x7, starting transfers between devices: 14.6 us -> 8.81 us  [exchange(): return lax.ppermute(array, 'stn', [(i, i ^ flip) for i in range(16)])]
    ppermute x7, waiting for transfers between devices: 2.22 us -> 7.85 us  [exchange(): return lax.ppermute(array, 'stn', [(i, i ^ flip) for i in range(16)])]
    unnamed x10 -> x4, local copies, waits for them, and re-layouts: 3.54 us -> 0.66 us
    div x2 -> x0, other arithmetic: 1.21 us -> none  [the longest x1 0.66 us: channelize(): scale = jnp.repeat(station_flags, 2).astype(jnp.float32) / math.sqrt(NCH)]
  transfers between devices with their start and end apart: 8 -> 8, of which waited for: 2 -> 7; matrix products, arithmetic and copies ran while one was open for 2% -> 0% of each run, Pallas kernels for 11% -> 14%
where the time goes in v2:
time: 63 us; the launch traced here: 62.6 us
  Pallas kernels  27.3 us (43%)
  waiting for transfers between devices  17.8 us (28%)
  starting transfers between devices  16.4 us (26%)
  local copies, waits for them, and re-layouts  0.75 us (1%)
    pallas_call x1, Pallas kernels, channelize(): pl.pallas_call(channelize_kernel, grid=(steps,), in_specs=[pl.BlockSpec((...  15.3 us
    pallas_call x3, Pallas kernels, correlate(): pl.pallas_call(functools.partial(correlate_kernel, count), grid=(CAP // B...  12 us
    all_to_all x1, waiting for transfers between devices, per_device(): lax.all_to_all(selected, ('stn', 'chan'), 0, 0, axis_index_groups=members...  9.93 us
    ppermute x7, starting transfers between devices, exchange(): return lax.ppermute(array, 'stn', [(i, i ^ flip) for i in range(16)])  8.81 us
    ppermute x7, waiting for transfers between devices, exchange(): return lax.ppermute(array, 'stn', [(i, i ^ flip) for i in range(16)])  7.85 us
    all_to_all x1, starting transfers between devices, per_device(): lax.all_to_all(selected, ('stn', 'chan'), 0, 0, axis_index_groups=members...  7.6 us
  transfers between devices with their start and end apart: 8, of which 7 were waited for; matrix products, arithmetic and copies ran while one was open for 0% of the time, Pallas kernels for 14%

profile of v2, /device:TPU:1, one launch (start us, length us, event | category | flops | bytes accessed | tf_op | source)
XLA Modules:
  0.0 62.6 jit_solution(11522517687652962099)
XLA Ops:
  0.0 15.3 %channelize.1 = bf16[2,8,16,8,128]{4,3,2,1,0:T(8,128)(2,1)} custom-call(bf16[2,31,8,8192]{3,2,1,0:T(8,128)(2,1)} %bitcast.20, f32[16,8192]{1,0:T(8,128)} %refs_1_.4, bf16[128,128]{1,0:T(8,128)(2,1)} %constant.91.clone.refs_2_, f32[2,64,128]{2,1,0:T(8,128)} %constant.93.clone.refs_3_, bf16[256,256]{1,0:T(8,128)(2,1)} %constant.92.clone.refs_4_, ...), custom_call_target="tpu_custom_call" | custom-call | tf_op jit(solution)/shard_map/channelize/pallas_call | solution.py:162
  15.3 7.6 %all-to-all-start = ((bf16[16,16,8,128]{3,2,1,0:T(8,128)(2,1)}), bf16[16,16,8,128]{3,2,1,0:T(8,128)(2,1)S(1)}, u32[]{:S(2)}, u32[]{:S(2)}) async-start(bf16[16,16,8,128]{3,2,1,0:T(8,128)(2,1)} %bitcast.21), calls=%async_computation | async-start | bytes 1048576 | tf_op jit(solution)/shard_map/all_to_all | solution.py:290
  23.0 9.9 %all-to-all-done = bf16[16,16,8,128]{3,2,1,0:T(8,128)(2,1)S(1)} async-done(((bf16[16,16,8,128]{3,2,1,0:T(8,128)(2,1)}), bf16[16,16,8,128]{3,2,1,0:T(8,128)(2,1)S(1)}, u32[]{:S(2)}, u32[]{:S(2)}) %all-to-all-start) | async-done | bytes 524320 | tf_op jit(solution)/shard_map/all_to_all | solution.py:290
  32.9 0.1 broadcast_select_fusion
  33.0 2.5 %collective-permute-start.3 = (bf16[8,16,8,128]{3,2,1,0:T(8,128)(2,1)S(1)}, bf16[8,16,8,128]{3,2,1,0:T(8,128)(2,1)S(1)}, u32[]{:S(2)}, u32[]{:S(2)}) collective-permute-start(bf16[8,16,8,128]{3,2,1,0:T(8,128)(2,1)S(1)} %get-tuple-element.15), channel_id=1, source_target_pairs={{0,8},{8,0},{16,24},{24,16},{32,40},{40,32},{48,56},{56,48},{64,72... | collective-permute-start | bytes 786440 | tf_op jit(solution)/shard_map/ppermute | solution.py:297
  35.5 0.1 broadcast_select_fusion.1
  35.5 3.8 %collective-permute-start.2 = (bf16[8,16,8,128]{3,2,1,0:T(8,128)(2,1)S(1)}, bf16[8,16,8,128]{3,2,1,0:T(8,128)(2,1)S(1)}, u32[]{:S(2)}, u32[]{:S(2)}) collective-permute-start(bf16[8,16,8,128]{3,2,1,0:T(8,128)(2,1)S(1)} %get-tuple-element.18), channel_id=1, source_target_pairs={{0,48},{8,56},{16,32},{24,40},{32,16},{40,24},{48,0},{56,8},{64,11... | collective-permute-start | bytes 786440 | tf_op jit(solution)/shard_map/ppermute | solution.py:297
  39.4 0.0 collective-permute-start.1
  39.4 0.1 pad_add_fusion.1.refs_0_
  39.4 0.7 %copy-done = s32[8]{0:T(128)S(1)} copy-done((s32[8]{0:T(128)S(1)}, s32[8]{0:T(128)}, u32[]{:S(2)}) %copy-start) | copy-done | bytes 56
  40.1 4.1 %correlate.3.refs_7_ = f32[9,64,64,128]{3,2,1,0:T(8,128)} custom-call(s32[4]{0:T(128)S(1)} %pad_add_fusion.1.refs_0_, s32[8]{0:T(128)S(1)} %copy-done, bf16[8,16,8,128]{3,2,1,0:T(8,128)(2,1)S(1)} %get-tuple-element.17.refs_2_.refs_3_, bf16[8,16,8,128]{3,2,1,0:T(8,128)(2,1)S(1)} %get-tuple-element.17.refs_2_.refs_3_, ...), custom_call_target="tpu_custom_call" | custom-call | tf_op jit(solution)/shard_map/correlate/pallas_call | solution.py:264
  44.2 1.8 %collective-permute-done.2.refs_5_ = bf16[8,16,8,128]{3,2,1,0:T(8,128)(2,1)S(1)} collective-permute-done((bf16[8,16,8,128]{3,2,1,0:T(8,128)(2,1)S(1)}, bf16[8,16,8,128]{3,2,1,0:T(8,128)(2,1)S(1)}, u32[]{:S(2)}, u32[]{:S(2)}) %collective-permute-start.2) | collective-permute-done | bytes 262176 | tf_op jit(solution)/shard_map/ppermute | solution.py:297
  46.0 0.9 %collective-permute-done.1.refs_3_ = bf16[8,16,8,128]{3,2,1,0:T(8,128)(2,1)S(1)} collective-permute-done((bf16[8,16,8,128]{3,2,1,0:T(8,128)(2,1)S(1)}, bf16[8,16,8,128]{3,2,1,0:T(8,128)(2,1)S(1)}, u32[]{:S(2)}, u32[]{:S(2)}) %collective-permute-start.1) | collective-permute-done | bytes 262176 | tf_op jit(solution)/shard_map/ppermute | solution.py:297
  46.9 1.1 %collective-permute-start.4 = (bf16[8,16,8,128]{3,2,1,0:T(8,128)(2,1)S(1)}, bf16[8,16,8,128]{3,2,1,0:T(8,128)(2,1)S(1)}, u32[]{:S(2)}, u32[]{:S(2)}) collective-permute-start(bf16[8,16,8,128]{3,2,1,0:T(8,128)(2,1)S(1)} %collective-permute-done.1.refs_3_), channel_id=1, source_target_pairs={{0,8},{8,0},{16,24},{24,16},{32,40},{40,32},{48,56},{56,48},{64,72... | collective-permute-start | bytes 786440 | tf_op jit(solution)/shard_map/ppermute | solution.py:297
  48.1 0.0 collective-permute-start.5
  48.1 0.1 stack.43.refs_0_
  48.2 1.1 %collective-permute-done.4.refs_4_ = bf16[8,16,8,128]{3,2,1,0:T(8,128)(2,1)S(1)} collective-permute-done((bf16[8,16,8,128]{3,2,1,0:T(8,128)(2,1)S(1)}, bf16[8,16,8,128]{3,2,1,0:T(8,128)(2,1)S(1)}, u32[]{:S(2)}, u32[]{:S(2)}) %collective-permute-start.4) | collective-permute-done | bytes 262176 | tf_op jit(solution)/shard_map/ppermute | solution.py:297
  49.2 0.4 collective-permute-done.5.refs_6_
  49.6 4.7 %correlate.4.refs_5_ = f32[9,64,64,128]{3,2,1,0:T(8,128)} custom-call(s32[5]{0:T(128)S(1)} %stack.43.refs_0_, s32[8]{0:T(128)S(1)} %copy-done.1, bf16[8,16,8,128]{3,2,1,0:T(8,128)(2,1)S(1)} %get-tuple-element.17.refs_2_.refs_3_, bf16[8,16,8,128]{3,2,1,0:T(8,128)(2,1)S(1)} %collective-permute-done.1.refs_3_, ...), custom_call_target="tpu_custom_call", output_to_operand_aliasing={{}: (7, {})} | custom-call | tf_op jit(solution)/shard_map/correlate/pallas_call | solution.py:264
  54.4 2.6 %collective-permute-done.refs_3_ = bf16[8,16,8,128]{3,2,1,0:T(8,128)(2,1)S(1)} collective-permute-done((bf16[8,16,8,128]{3,2,1,0:T(8,128)(2,1)S(1)}, bf16[8,16,8,128]{3,2,1,0:T(8,128)(2,1)S(1)}, u32[]{:S(2)}, u32[]{:S(2)}) %collective-permute-start) | collective-permute-done | bytes 262176 | tf_op jit(solution)/shard_map/ppermute | solution.py:297
  56.9 1.4 %collective-permute-start.6 = (bf16[8,16,8,128]{3,2,1,0:T(8,128)(2,1)S(1)}, bf16[8,16,8,128]{3,2,1,0:T(8,128)(2,1)S(1)}, u32[]{:S(2)}, u32[]{:S(2)}) collective-permute-start(bf16[8,16,8,128]{3,2,1,0:T(8,128)(2,1)S(1)} %collective-permute-done.refs_3_), channel_id=1, source_target_pairs={{0,8},{8,0},{16,24},{24,16},{32,40},{40,32},{48,56},{56,48},{64,72... | collective-permute-start | bytes 786440 | tf_op jit(solution)/shard_map/ppermute | solution.py:297
  58.3 0.1 pad_add_fusion.refs_0_
  58.4 1.1 %collective-permute-done.6.refs_4_ = bf16[8,16,8,128]{3,2,1,0:T(8,128)(2,1)S(1)} collective-permute-done((bf16[8,16,8,128]{3,2,1,0:T(8,128)(2,1)S(1)}, bf16[8,16,8,128]{3,2,1,0:T(8,128)(2,1)S(1)}, u32[]{:S(2)}, u32[]{:S(2)}) %collective-permute-start.6) | collective-permute-done | bytes 262176 | tf_op jit(solution)/shard_map/ppermute | solution.py:297
  59.5 3.1 %correlate.5 = f32[9,64,64,128]{3,2,1,0:T(8,128)} custom-call(s32[3]{0:T(128)S(1)} %pad_add_fusion.refs_0_, s32[8]{0:T(128)S(1)} %copy-done.1, bf16[8,16,8,128]{3,2,1,0:T(8,128)(2,1)S(1)} %get-tuple-element.17.refs_2_.refs_3_, bf16[8,16,8,128]{3,2,1,0:T(8,128)(2,1)S(1)} %collective-permute-done.refs_3_, ...), custom_call_target="tpu_custom_call", output_to_operand_aliasing={{}: (5, {})} | custom-call | tf_op jit(solution)/shard_map/correlate/pallas_call | solution.py:264
  (5 shorter events, 0.0 us)
Async XLA Ops:
  0.0 49.6 %copy-start.1 = (s32[8]{0:T(128)S(1)}, s32[8]{0:T(128)}, u32[]{:S(2)}) copy-start(s32[8]{0:T(128)} %refs_1_.7) | copy-start | bytes 100
  15.3 17.6 %all-to-all-start = ((bf16[16,16,8,128]{3,2,1,0:T(8,128)(2,1)}), bf16[16,16,8,128]{3,2,1,0:T(8,128)(2,1)S(1)}, u32[]{:S(2)}, u32[]{:S(2)}) async-start(bf16[16,16,8,128]{3,2,1,0:T(8,128)(2,1)} %bitcast.21), calls=%async_computation | async-start | bytes 1048576 | tf_op jit(solution)/shard_map/all_to_all | solution.py:290
  33.0 6.5 %collective-permute-start.3 = (bf16[8,16,8,128]{3,2,1,0:T(8,128)(2,1)S(1)}, bf16[8,16,8,128]{3,2,1,0:T(8,128)(2,1)S(1)}, u32[]{:S(2)}, u32[]{:S(2)}) collective-permute-start(bf16[8,16,8,128]{3,2,1,0:T(8,128)(2,1)S(1)} %get-tuple-element.15), channel_id=1, source_target_pairs={{0,8},{8,0},{16,24},{24,16},{32,40},{40,32},{48,56},{56,48},{64,72... | collective-permute-start | bytes 786440 | tf_op jit(solution)/shard_map/ppermute | solution.py:297
  35.5 10.5 %collective-permute-start.2 = (bf16[8,16,8,128]{3,2,1,0:T(8,128)(2,1)S(1)}, bf16[8,16,8,128]{3,2,1,0:T(8,128)(2,1)S(1)}, u32[]{:S(2)}, u32[]{:S(2)}) collective-permute-start(bf16[8,16,8,128]{3,2,1,0:T(8,128)(2,1)S(1)} %get-tuple-element.18), channel_id=1, source_target_pairs={{0,48},{8,56},{16,32},{24,40},{32,16},{40,24},{48,0},{56,8},{64,11... | collective-permute-start | bytes 786440 | tf_op jit(solution)/shard_map/ppermute | solution.py:297
  39.4 7.6 %collective-permute-start.1 = (bf16[8,16,8,128]{3,2,1,0:T(8,128)(2,1)S(1)}, bf16[8,16,8,128]{3,2,1,0:T(8,128)(2,1)S(1)}, u32[]{:S(2)}, u32[]{:S(2)}) collective-permute-start(bf16[8,16,8,128]{3,2,1,0:T(8,128)(2,1)S(1)} %get-tuple-element.19), channel_id=1, source_target_pairs={{0,16},{8,24},{16,0},{24,8},{32,48},{40,56},{48,32},{56,40},{64,80... | collective-permute-start | bytes 786440 | tf_op jit(solution)/shard_map/ppermute | solution.py:297
  39.4 0.7 %copy-start = (s32[8]{0:T(128)S(1)}, s32[8]{0:T(128)}, u32[]{:S(2)}) copy-start(s32[8]{0:T(128)} %refs_1_.7) | copy-start | bytes 100
  46.9 2.3 %collective-permute-start.4 = (bf16[8,16,8,128]{3,2,1,0:T(8,128)(2,1)S(1)}, bf16[8,16,8,128]{3,2,1,0:T(8,128)(2,1)S(1)}, u32[]{:S(2)}, u32[]{:S(2)}) collective-permute-start(bf16[8,16,8,128]{3,2,1,0:T(8,128)(2,1)S(1)} %collective-permute-done.1.refs_3_), channel_id=1, source_target_pairs={{0,8},{8,0},{16,24},{24,16},{32,40},{40,32},{48,56},{56,48},{64,72... | collective-permute-start | bytes 786440 | tf_op jit(solution)/shard_map/ppermute | solution.py:297
  48.1 1.5 %collective-permute-start.5 = (bf16[8,16,8,128]{3,2,1,0:T(8,128)(2,1)S(1)}, bf16[8,16,8,128]{3,2,1,0:T(8,128)(2,1)S(1)}, u32[]{:S(2)}, u32[]{:S(2)}) collective-permute-start(bf16[8,16,8,128]{3,2,1,0:T(8,128)(2,1)S(1)} %collective-permute-done.2.refs_5_), channel_id=1, source_target_pairs={{0,8},{8,0},{16,24},{24,16},{32,40},{40,32},{48,56},{56,48},{64,72... | collective-permute-start | bytes 786440 | tf_op jit(solution)/shard_map/ppermute | solution.py:297
  48.1 8.9 %collective-permute-start = (bf16[8,16,8,128]{3,2,1,0:T(8,128)(2,1)S(1)}, bf16[8,16,8,128]{3,2,1,0:T(8,128)(2,1)S(1)}, u32[]{:S(2)}, u32[]{:S(2)}) collective-permute-start(bf16[8,16,8,128]{3,2,1,0:T(8,128)(2,1)S(1)} %get-tuple-element.20), channel_id=1, source_target_pairs={{0,32},{8,40},{16,48},{24,56},{32,0},{40,8},{48,16},{56,24},{64,96... | collective-permute-start | bytes 786440 | tf_op jit(solution)/shard_map/ppermute | solution.py:297
  56.9 2.5 %collective-permute-start.6 = (bf16[8,16,8,128]{3,2,1,0:T(8,128)(2,1)S(1)}, bf16[8,16,8,128]{3,2,1,0:T(8,128)(2,1)S(1)}, u32[]{:S(2)}, u32[]{:S(2)}) collective-permute-start(bf16[8,16,8,128]{3,2,1,0:T(8,128)(2,1)S(1)} %collective-permute-done.refs_3_), channel_id=1, source_target_pairs={{0,8},{8,0},{16,24},{24,16},{32,40},{40,32},{48,56},{56,48},{64,72... | collective-permute-start | bytes 786440 | tf_op jit(solution)/shard_map/ppermute | solution.py:297

commit v3 on v2

--- a/solution.py
+++ b/solution.py
@@ -187,34 +187,17 @@
     )(volts, filter_taps, first_w, twid, second_w, subband_lists, station_flags)
 
 
-BSLOTS = 8
-
-
 def correlate_kernel(count, *refs):
     places, counts, own = refs[:3]
     others = refs[3 : 3 + count]
     out, results, sems = refs[-3:]
-    step = pl.program_id(0)
-    steps = pl.num_programs(0)
     lane = lax.broadcasted_iota(jnp.int32, (64, LANES), 1)
     real_lane = lane // SUBW % 2 == 0
-    buf = step % 2
-
-    def copies(at, slot):
-        rows = pl.ds(at * BSLOTS * SUBW, BSLOTS * SUBW)
-        return [
-            pltpu.make_async_copy(results.at[slot, n], out.at[places[n + 1], rows], sems.at[slot, n])
-            for n in range(count)
-        ]
-
-    @pl.when(step >= 2)
-    def reuse():
-        for copy in copies(step - 2, buf):
-            copy.wait()
-
-    for k in range(BSLOTS):
-        factor = jnp.where(step * BSLOTS + k < counts[places[0]], 1.0 / SPECTRA, 0.0)
-        mine = own[:, k].astype(jnp.float32).reshape(64, LANES) * factor
+    zero = jnp.zeros((64, LANES), jnp.bfloat16)
+
+    def one_slot(slot, carry):
+        factor = jnp.where(slot < counts[places[0]], 1.0 / SPECTRA, 0.0)
+        mine = own[:, slot].astype(jnp.float32).reshape(64, LANES) * factor
         crossed = jnp.where(real_lane, pltpu.roll(mine, LANES - SUBW, 1), -pltpu.roll(mine, SUBW, 1))
         left = jnp.concatenate(
             [
@@ -225,11 +208,11 @@
             ],
             axis=0,
         )
-        zero = jnp.zeros((64, LANES), jnp.bfloat16)
+        rows = pl.ds(slot * SUBW, SUBW)
         for at in range(0, count, 2):
             right = []
             for n in range(at, min(at + 2, count)):
-                block = others[n][:, k].reshape(64, LANES)
+                block = others[n][:, slot].reshape(64, LANES)
                 right += [jnp.concatenate([block, zero], axis=1), jnp.concatenate([zero, block], axis=1)]
             right = jnp.concatenate(right, axis=0)
             product = lax.dot_general(
@@ -237,25 +220,25 @@
             )
             for n in range(at, min(at + 2, count)):
                 piece = product[:, (n - at) * 128 : (n - at + 1) * 128]
-                results[buf, n, k * SUBW : (k + 1) * SUBW] = piece.reshape(SUBW, 64, 128)
-
-    for copy in copies(step, buf):
-        copy.start()
-
-    @pl.when(step == steps - 1)
-    def finish():
-        for copy in copies(step - 1, 1 - buf) + copies(step, buf):
-            copy.wait()
+                results[n, rows] = piece.reshape(SUBW, 64, 128)
+        for n in range(count):
+            pltpu.make_async_copy(results.at[n, rows], out.at[places[n + 1], rows], sems.at[n]).start()
+        return carry
+
+    lax.fori_loop(0, CAP, one_slot, 0, unroll=CUNROLL)
+    for n in range(count):
+        pltpu.make_async_copy(results.at[n], out.at[places[n + 1]], sems.at[n]).wait()
+
+
+CUNROLL = 4
 
 
 def correlate(total, group, counts, own, pairs):
     places = jnp.stack([group] + [distance for distance, _ in pairs]).astype(jnp.int32)
     others = [block for _, block in pairs]
     count = len(others)
-    block = pl.BlockSpec((8, BSLOTS, LOCAL, LANES), lambda n: (0, n, 0, 0))
-    shape = jax.ShapeDtypeStruct((9, CAP * SUBW, 64, 128), jnp.float32)
     args = [places, counts, own, *others]
-    specs = [pl.BlockSpec(memory_space=pltpu.SMEM)] * 2 + [block] * (1 + count)
+    specs = [pl.BlockSpec(memory_space=pltpu.SMEM)] * 2 + [pl.BlockSpec(memory_space=pltpu.VMEM)] * (1 + count)
     aliases = {}
     if total is not None:
         aliases = {len(args): 0}
@@ -263,13 +246,12 @@
         specs.append(pl.BlockSpec(memory_space=pl.ANY))
     return pl.pallas_call(
         functools.partial(correlate_kernel, count),
-        grid=(CAP // BSLOTS,),
         in_specs=specs,
         out_specs=pl.BlockSpec(memory_space=pl.ANY),
-        out_shape=shape,
+        out_shape=jax.ShapeDtypeStruct((9, CAP * SUBW, 64, 128), jnp.float32),
         scratch_shapes=[
-            pltpu.VMEM((2, count, BSLOTS * SUBW, 64, 128), jnp.float32),
-            pltpu.SemaphoreType.DMA((2, count)),
+            pltpu.VMEM((count, CAP * SUBW, 64, 128), jnp.float32),
+            pltpu.SemaphoreType.DMA((count,)),
         ],
         input_output_aliases=aliases,
         compiler_params=pltpu.CompilerParams(vmem_limit_bytes=VMEM),
@@ -308,13 +290,11 @@
     ahead = {flip: 2 * ((col ^ flip) - col + 4) % 8 for flip in (1, 2, 3)}
     join = functools.partial(correlate, group=group, counts=subband_counts, own=own)
     total = join(None, pairs=[(0 * core, own), (0 * core + 8, far), (1 + 6 * core, spare)])
-    for flips in ((1, 3), (2,)):
-        arrived = [moved[flip] for flip in flips]
-        *arrived, total = lax.optimization_barrier((*arrived, total))
-        pairs = []
-        for flip, block in zip(flips, arrived):
-            pairs += [(ahead[flip], block), (ahead[flip] + side, exchange(block, 1))]
-        total = join(total, pairs=pairs)
+    *arrived, total = lax.optimization_barrier((*(moved[flip] for flip in (1, 3, 2)), total))
+    pairs = []
+    for flip, block in zip((1, 3, 2), arrived):
+        pairs += [(ahead[flip], block), (ahead[flip] + side, exchange(block, 1))]
+    total = join(total, pairs=pairs)
     return total[None]
 
 

time: 63 us -> 60.6 us (0.962)
  Pallas kernels: 27.3 us -> 24.2 us
  waiting for transfers between devices: 17.8 us -> 19.1 us
    pallas_call x3 -> x2, Pallas kernels: 12 us -> 8.89 us  [correlate(): pl.pallas_call(functools.partial(correlate_kernel, count), in_specs=specs...]
    ppermute x7, waiting for transfers between devices: 7.85 us -> 9.22 us  [exchange(): return lax.ppermute(array, 'stn', [(i, i ^ flip) for i in range(16)])]
  transfers between devices with their start and end apart: 8 -> 8, of which waited for: 7 -> 7; matrix products, arithmetic and copies ran while one was open for 0% -> 0% of each run, Pallas kernels for 14% -> 6%
where the time goes in v3:
time: 60.6 us; the launch traced here: 60.2 us
  Pallas kernels  24.2 us (40%)
  waiting for transfers between devices  19.1 us (32%)
  starting transfers between devices  15.8 us (26%)
  local copies, waits for them, and re-layouts  0.75 us (1%)
    pallas_call x1, Pallas kernels, channelize(): pl.pallas_call(channelize_kernel, grid=(steps,), in_specs=[pl.BlockSpec((...  15.3 us
    all_to_all x1, waiting for transfers between devices, per_device(): lax.all_to_all(selected, ('stn', 'chan'), 0, 0, axis_index_groups=members...  9.93 us
    ppermute x7, waiting for transfers between devices, exchange(): return lax.ppermute(array, 'stn', [(i, i ^ flip) for i in range(16)])  9.22 us
    pallas_call x2, Pallas kernels, correlate(): pl.pallas_call(functools.partial(correlate_kernel, count), in_specs=specs...  8.89 us
    ppermute x7, starting transfers between devices, exchange(): return lax.ppermute(array, 'stn', [(i, i ^ flip) for i in range(16)])  8.21 us
    all_to_all x1, starting transfers between devices, per_device(): lax.all_to_all(selected, ('stn', 'chan'), 0, 0, axis_index_groups=members...  7.6 us
  transfers between devices with their start and end apart: 8, of which 7 were waited for; matrix products, arithmetic and copies ran while one was open for 0% of the time, Pallas kernels for 6%

profile of v3, /device:TPU:1, one launch (start us, length us, event | category | flops | bytes accessed | tf_op | source)
XLA Modules:
  0.0 60.2 jit_solution(16250542227749545096)
XLA Ops:
  0.0 15.3 %channelize.1 = bf16[2,8,16,8,128]{4,3,2,1,0:T(8,128)(2,1)} custom-call(bf16[2,31,8,8192]{3,2,1,0:T(8,128)(2,1)} %bitcast.20, f32[16,8192]{1,0:T(8,128)} %refs_1_.3, bf16[128,128]{1,0:T(8,128)(2,1)} %constant.91.clone.refs_2_, f32[2,64,128]{2,1,0:T(8,128)} %constant.93.clone.refs_3_, bf16[256,256]{1,0:T(8,128)(2,1)} %constant.92.clone.refs_4_, ...), custom_call_target="tpu_custom_call" | custom-call | tf_op jit(solution)/shard_map/channelize/pallas_call | solution.py:162
  15.3 7.6 %all-to-all-start = ((bf16[16,16,8,128]{3,2,1,0:T(8,128)(2,1)}), bf16[16,16,8,128]{3,2,1,0:T(8,128)(2,1)S(1)}, u32[]{:S(2)}, u32[]{:S(2)}) async-start(bf16[16,16,8,128]{3,2,1,0:T(8,128)(2,1)} %bitcast.21), calls=%async_computation | async-start | bytes 1048576 | tf_op jit(solution)/shard_map/all_to_all | solution.py:272
  23.0 9.9 %all-to-all-done = bf16[16,16,8,128]{3,2,1,0:T(8,128)(2,1)S(1)} async-done(((bf16[16,16,8,128]{3,2,1,0:T(8,128)(2,1)}), bf16[16,16,8,128]{3,2,1,0:T(8,128)(2,1)S(1)}, u32[]{:S(2)}, u32[]{:S(2)}) %all-to-all-start) | async-done | bytes 524320 | tf_op jit(solution)/shard_map/all_to_all | solution.py:272
  32.9 0.1 broadcast_select_fusion
  33.0 2.5 %collective-permute-start.3 = (bf16[8,16,8,128]{3,2,1,0:T(8,128)(2,1)S(1)}, bf16[8,16,8,128]{3,2,1,0:T(8,128)(2,1)S(1)}, u32[]{:S(2)}, u32[]{:S(2)}) collective-permute-start(bf16[8,16,8,128]{3,2,1,0:T(8,128)(2,1)S(1)} %get-tuple-element.13), channel_id=1, source_target_pairs={{0,8},{8,0},{16,24},{24,16},{32,40},{40,32},{48,56},{56,48},{64,72... | collective-permute-start | bytes 786440 | tf_op jit(solution)/shard_map/ppermute | solution.py:279
  35.5 0.1 broadcast_select_fusion.1
  35.5 3.7 %collective-permute-start.2 = (bf16[8,16,8,128]{3,2,1,0:T(8,128)(2,1)S(1)}, bf16[8,16,8,128]{3,2,1,0:T(8,128)(2,1)S(1)}, u32[]{:S(2)}, u32[]{:S(2)}) collective-permute-start(bf16[8,16,8,128]{3,2,1,0:T(8,128)(2,1)S(1)} %get-tuple-element.16), channel_id=1, source_target_pairs={{0,32},{8,40},{16,48},{24,56},{32,0},{40,8},{48,16},{56,24},{64,96... | collective-permute-start | bytes 786440 | tf_op jit(solution)/shard_map/ppermute | solution.py:279
  39.2 0.4 collective-permute-start.1
  39.6 0.3 collective-permute-start
  39.9 0.1 pad_add_fusion.refs_0_
  40.0 0.0 collective-permute-done.3.refs_5_
  40.0 0.7 %copy-done = s32[8]{0:T(128)S(1)} copy-done((s32[8]{0:T(128)S(1)}, s32[8]{0:T(128)}, u32[]{:S(2)}) %copy-start) | copy-done | bytes 56
  40.7 3.5 %correlate.2.refs_9_ = f32[9,64,64,128]{3,2,1,0:T(8,128)} custom-call(s32[4]{0:T(128)S(1)} %pad_add_fusion.refs_0_, s32[8]{0:T(128)S(1)} %copy-done, bf16[8,16,8,128]{3,2,1,0:T(8,128)(2,1)S(1)} %get-tuple-element.15.refs_2_.refs_3_, bf16[8,16,8,128]{3,2,1,0:T(8,128)(2,1)S(1)} %get-tuple-element.15.refs_2_.refs_3_, ...), custom_call_target="tpu_custom_call" | custom-call | tf_op jit(solution)/shard_map/correlate/pallas_call | solution.py:247
  44.1 1.8 %collective-permute-done.2.refs_7_ = bf16[8,16,8,128]{3,2,1,0:T(8,128)(2,1)S(1)} collective-permute-done((bf16[8,16,8,128]{3,2,1,0:T(8,128)(2,1)S(1)}, bf16[8,16,8,128]{3,2,1,0:T(8,128)(2,1)S(1)}, u32[]{:S(2)}, u32[]{:S(2)}) %collective-permute-start.2) | collective-permute-done | bytes 262176 | tf_op jit(solution)/shard_map/ppermute | solution.py:279
  45.9 5.7 %collective-permute-done.1.refs_5_ = bf16[8,16,8,128]{3,2,1,0:T(8,128)(2,1)S(1)} collective-permute-done((bf16[8,16,8,128]{3,2,1,0:T(8,128)(2,1)S(1)}, bf16[8,16,8,128]{3,2,1,0:T(8,128)(2,1)S(1)}, u32[]{:S(2)}, u32[]{:S(2)}) %collective-permute-start.1) | collective-permute-done | bytes 262176 | tf_op jit(solution)/shard_map/ppermute | solution.py:279
  51.6 0.4 collective-permute-done.refs_3_
  52.0 0.8 %collective-permute-start.4 = (bf16[8,16,8,128]{3,2,1,0:T(8,128)(2,1)S(1)}, bf16[8,16,8,128]{3,2,1,0:T(8,128)(2,1)S(1)}, u32[]{:S(2)}, u32[]{:S(2)}) collective-permute-start(bf16[8,16,8,128]{3,2,1,0:T(8,128)(2,1)S(1)} %collective-permute-done.refs_3_), channel_id=1, source_target_pairs={{0,8},{8,0},{16,24},{24,16},{32,40},{40,32},{48,56},{56,48},{64,72... | collective-permute-start | bytes 786440 | tf_op jit(solution)/shard_map/ppermute | solution.py:279
  52.9 0.0 collective-permute-start.5
  52.9 0.5 collective-permute-start.6
  53.4 0.1 stack.38.refs_0_
  53.5 0.6 collective-permute-done.4.refs_4_
  54.0 0.4 collective-permute-done.5.refs_6_
  54.4 0.4 collective-permute-done.6.refs_8_
  54.8 5.4 %correlate.3 = f32[9,64,64,128]{3,2,1,0:T(8,128)} custom-call(s32[7]{0:T(128)S(1)} %stack.38.refs_0_, s32[8]{0:T(128)S(1)} %copy-done.1, bf16[8,16,8,128]{3,2,1,0:T(8,128)(2,1)S(1)} %get-tuple-element.15.refs_2_.refs_3_, bf16[8,16,8,128]{3,2,1,0:T(8,128)(2,1)S(1)} %collective-permute-done.refs_3_, ...), custom_call_target="tpu_custom_call", output_to_operand_aliasing={{}: (9, {})} | custom-call | tf_op jit(solution)/shard_map/correlate/pallas_call | solution.py:247
  (3 shorter events, 0.0 us)
Async XLA Ops:
  0.0 54.8 %copy-start.1 = (s32[8]{0:T(128)S(1)}, s32[8]{0:T(128)}, u32[]{:S(2)}) copy-start(s32[8]{0:T(128)} %refs_1_.5) | copy-start | bytes 100
  15.3 17.6 %all-to-all-start = ((bf16[16,16,8,128]{3,2,1,0:T(8,128)(2,1)}), bf16[16,16,8,128]{3,2,1,0:T(8,128)(2,1)S(1)}, u32[]{:S(2)}, u32[]{:S(2)}) async-start(bf16[16,16,8,128]{3,2,1,0:T(8,128)(2,1)} %bitcast.21), calls=%async_computation | async-start | bytes 1048576 | tf_op jit(solution)/shard_map/all_to_all | solution.py:272
  33.0 7.0 %collective-permute-start.3 = (bf16[8,16,8,128]{3,2,1,0:T(8,128)(2,1)S(1)}, bf16[8,16,8,128]{3,2,1,0:T(8,128)(2,1)S(1)}, u32[]{:S(2)}, u32[]{:S(2)}) collective-permute-start(bf16[8,16,8,128]{3,2,1,0:T(8,128)(2,1)S(1)} %get-tuple-element.13), channel_id=1, source_target_pairs={{0,8},{8,0},{16,24},{24,16},{32,40},{40,32},{48,56},{56,48},{64,72... | collective-permute-start | bytes 786440 | tf_op jit(solution)/shard_map/ppermute | solution.py:279
  35.5 10.4 %collective-permute-start.2 = (bf16[8,16,8,128]{3,2,1,0:T(8,128)(2,1)S(1)}, bf16[8,16,8,128]{3,2,1,0:T(8,128)(2,1)S(1)}, u32[]{:S(2)}, u32[]{:S(2)}) collective-permute-start(bf16[8,16,8,128]{3,2,1,0:T(8,128)(2,1)S(1)} %get-tuple-element.16), channel_id=1, source_target_pairs={{0,32},{8,40},{16,48},{24,56},{32,0},{40,8},{48,16},{56,24},{64,96... | collective-permute-start | bytes 786440 | tf_op jit(solution)/shard_map/ppermute | solution.py:279
  39.2 12.4 %collective-permute-start.1 = (bf16[8,16,8,128]{3,2,1,0:T(8,128)(2,1)S(1)}, bf16[8,16,8,128]{3,2,1,0:T(8,128)(2,1)S(1)}, u32[]{:S(2)}, u32[]{:S(2)}) collective-permute-start(bf16[8,16,8,128]{3,2,1,0:T(8,128)(2,1)S(1)} %get-tuple-element.17), channel_id=1, source_target_pairs={{0,48},{8,56},{16,32},{24,40},{32,16},{40,24},{48,0},{56,8},{64,11... | collective-permute-start | bytes 786440 | tf_op jit(solution)/shard_map/ppermute | solution.py:279
  39.6 12.4 %collective-permute-start = (bf16[8,16,8,128]{3,2,1,0:T(8,128)(2,1)S(1)}, bf16[8,16,8,128]{3,2,1,0:T(8,128)(2,1)S(1)}, u32[]{:S(2)}, u32[]{:S(2)}) collective-permute-start(bf16[8,16,8,128]{3,2,1,0:T(8,128)(2,1)S(1)} %get-tuple-element.18), channel_id=1, source_target_pairs={{0,16},{8,24},{16,0},{24,8},{32,48},{40,56},{48,32},{56,40},{64,80... | collective-permute-start | bytes 786440 | tf_op jit(solution)/shard_map/ppermute | solution.py:279
  40.0 0.7 %copy-start = (s32[8]{0:T(128)S(1)}, s32[8]{0:T(128)}, u32[]{:S(2)}) copy-start(s32[8]{0:T(128)} %refs_1_.5) | copy-start | bytes 100
  52.0 2.0 %collective-permute-start.4 = (bf16[8,16,8,128]{3,2,1,0:T(8,128)(2,1)S(1)}, bf16[8,16,8,128]{3,2,1,0:T(8,128)(2,1)S(1)}, u32[]{:S(2)}, u32[]{:S(2)}) collective-permute-start(bf16[8,16,8,128]{3,2,1,0:T(8,128)(2,1)S(1)} %collective-permute-done.refs_3_), channel_id=1, source_target_pairs={{0,8},{8,0},{16,24},{24,16},{32,40},{40,32},{48,56},{56,48},{64,72... | collective-permute-start | bytes 786440 | tf_op jit(solution)/shard_map/ppermute | solution.py:279
  52.9 1.5 %collective-permute-start.5 = (bf16[8,16,8,128]{3,2,1,0:T(8,128)(2,1)S(1)}, bf16[8,16,8,128]{3,2,1,0:T(8,128)(2,1)S(1)}, u32[]{:S(2)}, u32[]{:S(2)}) collective-permute-start(bf16[8,16,8,128]{3,2,1,0:T(8,128)(2,1)S(1)} %collective-permute-done.1.refs_5_), channel_id=1, source_target_pairs={{0,8},{8,0},{16,24},{24,16},{32,40},{40,32},{48,56},{56,48},{64,72... | collective-permute-start | bytes 786440 | tf_op jit(solution)/shard_map/ppermute | solution.py:279
  52.9 1.9 %collective-permute-start.6 = (bf16[8,16,8,128]{3,2,1,0:T(8,128)(2,1)S(1)}, bf16[8,16,8,128]{3,2,1,0:T(8,128)(2,1)S(1)}, u32[]{:S(2)}, u32[]{:S(2)}) collective-permute-start(bf16[8,16,8,128]{3,2,1,0:T(8,128)(2,1)S(1)} %collective-permute-done.2.refs_7_), channel_id=1, source_target_pairs={{0,8},{8,0},{16,24},{24,16},{32,40},{40,32},{48,56},{56,48},{64,72... | collective-permute-start | bytes 786440 | tf_op jit(solution)/shard_map/ppermute | solution.py:279

commit v4 on v3

--- a/solution.py
+++ b/solution.py
@@ -19,7 +19,9 @@
 SEGMENTS = SPECTRA + TAPS - 1
 LOCAL = 8
 LANES = SPECTRA * 2 * SUBW
-CHUNK = 1024
+CHUNKS = (256, 256, 512, 1024, 2048, 2048, 2048)
+FUNROLL = 2
+DIRECT = 4
 PITCH = FIRST + 8
 GROUP = 8
 UNROLL = 8
@@ -36,11 +38,39 @@
     return np.block([[cosine, -sine], [sine, cosine]])
 
 
+def split_taps(taps):
+    half = len(taps) // 2
+    if len(taps) <= DIRECT:
+        return taps
+    low, high = taps[:half], taps[half:]
+    return split_taps(low), split_taps(high), split_taps([a + b for a, b in zip(low, high)])
+
+
+def sliding(tree, values, start=None):
+    length = (len(values) + 1) // 2
+    if isinstance(tree, list):
+        totals = []
+        for t in range(length):
+            total = None if start is None else start[t]
+            for j in range(length):
+                term = tree[j] * values[t + j]
+                total = term if total is None else total + term
+            totals.append(total)
+        return totals
+    low, high, both = tree
+    half = length // 2
+    span = range(length - 1)
+    shared = sliding(both, values[half : half + length - 1])
+    first = shared if start is None else [a + b for a, b in zip(start[:half], shared)]
+    second = shared if start is None else [a + b for a, b in zip(start[half:], shared)]
+    return sliding(low, [values[n] - values[n + half] for n in span], first) + sliding(
+        high, [values[n + length] - values[n + half] for n in span], second
+    )
+
+
 def channelize_kernel(*refs):
-    volts, taps, first_hbm, twid_hbm, second_hbm, lists, flags, out = refs[:8]
-    frames, picked, turned, first_w, twid, second_w, sems = refs[8:]
-    step = pl.program_id(0)
-    per_step = CHUNK // SECOND
+    volts_hbm, taps_hbm, first_hbm, twid_hbm, second_hbm, lists, flags, out = refs[:8]
+    frames, picked, turned, first_w, twid, second_w, volts, taps, sems, fetched = refs[8:]
 
     copies = [
         pltpu.make_async_copy(source, target, sems.at[n])
@@ -49,101 +79,108 @@
         )
     ]
 
-    @pl.when(step == 0)
-    def fetch():
-        for copy in copies:
+    starts = [sum(CHUNKS[:n]) for n in range(len(CHUNKS))]
+
+    def pieces(n):
+        lanes = pl.ds(starts[n], CHUNKS[n])
+        return (
+            pltpu.make_async_copy(taps_hbm.at[:, lanes], taps.at[:, lanes], fetched.at[n, 0]),
+            pltpu.make_async_copy(
+                volts_hbm.at[:, :, :, lanes], volts.at[:, :, :, lanes], fetched.at[n, 1]
+            ),
+        )
+
+    for n in range(len(CHUNKS)):
+        for copy in pieces(n):
             copy.start()
+    for copy in copies:
+        copy.start()
 
     def filter_one(at, carry):
         lanes = pl.ds(pl.multiple_of(at * SECOND, SECOND), SECOND)
-        row = step * per_step + at
+        row = at
         coeffs = [jnp.broadcast_to(taps[j : j + 1, lanes], (LOCAL, SECOND)) for j in range(TAPS)]
+        tree = split_taps(coeffs)
         for part in range(2):
-            sums = {}
-            for seg in range(SEGMENTS):
-                value = volts[part, seg, :, lanes].astype(jnp.float32)
-                for j in range(TAPS):
-                    t = seg - j
-                    if 0 <= t < SPECTRA:
-                        term = coeffs[j] * value
-                        sums[t] = sums[t] + term if t in sums else term
-                if seg >= TAPS - 1:
-                    t = seg - TAPS + 1
-                    frames[part, t, pl.ds(row, LOCAL, stride=PITCH), :] = sums.pop(t)
+            values = [volts[part, seg, :, lanes].astype(jnp.float32) for seg in range(SEGMENTS)]
+            for t, total in enumerate(sliding(tree, values)):
+                frames[part, t, pl.ds(row, LOCAL, stride=PITCH), :] = total
         return carry
 
-    lax.fori_loop(0, per_step, filter_one, 0, unroll=2)
-
-    @pl.when(step == pl.num_programs(0) - 1)
-    def transform():
-        for copy in copies:
+    for n in range(len(CHUNKS)):
+        for copy in pieces(n):
             copy.wait()
-        spread = lax.broadcasted_iota(jnp.int32, (CAP, 128), 1) % CAP == lax.broadcasted_iota(
-            jnp.int32, (CAP, 128), 0
-        )
-        spread = spread.astype(jnp.bfloat16)
-        diagonal = lax.broadcasted_iota(jnp.int32, (8, 128), 1) // CAP == lax.broadcasted_iota(
-            jnp.int32, (8, 128), 0
-        )
-
-        def along_lanes(numbers):
-            full = jnp.dot(numbers.astype(jnp.bfloat16), spread, preferred_element_type=jnp.float32)
-            return jnp.sum(jnp.where(diagonal, full, 0.0), axis=0, keepdims=True).astype(jnp.int32)
-
-        number_m = along_lanes(lists[...] // (FIRST // SUBW))
-        number_k = along_lanes(lists[...] % (FIRST // SUBW))
-        onehot = (lax.broadcasted_iota(jnp.int32, (SECOND, 128), 0) == number_m).astype(jnp.bfloat16)
-        chosen = jnp.concatenate(
+        first_row = starts[n] // SECOND
+        lax.fori_loop(first_row, first_row + CHUNKS[n] // SECOND, filter_one, 0, unroll=FUNROLL)
+
+    for copy in copies:
+        copy.wait()
+    spread = lax.broadcasted_iota(jnp.int32, (CAP, 128), 1) % CAP == lax.broadcasted_iota(
+        jnp.int32, (CAP, 128), 0
+    )
+    spread = spread.astype(jnp.bfloat16)
+    diagonal = lax.broadcasted_iota(jnp.int32, (8, 128), 1) // CAP == lax.broadcasted_iota(
+        jnp.int32, (8, 128), 0
+    )
+
+    def along_lanes(numbers):
+        full = jnp.dot(numbers.astype(jnp.bfloat16), spread, preferred_element_type=jnp.float32)
+        return jnp.sum(jnp.where(diagonal, full, 0.0), axis=0, keepdims=True).astype(jnp.int32)
+
+    number_m = along_lanes(lists[...] // (FIRST // SUBW))
+    number_k = along_lanes(lists[...] % (FIRST // SUBW))
+    onehot = (lax.broadcasted_iota(jnp.int32, (SECOND, 128), 0) == number_m).astype(jnp.bfloat16)
+    chosen = jnp.concatenate(
+        [
+            jnp.dot(second_w[:, q * SECOND : (q + 1) * SECOND], onehot, preferred_element_type=jnp.float32)
+            for q in range(2)
+        ],
+        axis=1,
+    ).astype(jnp.bfloat16)
+    half = lax.broadcasted_iota(jnp.int32, (8, 128), 0) // SUBW
+    masks = [number_k == 2 * v + half for v in range(FIRST // 8)]
+    low = half == 0
+    group = GROUP
+
+    def one(index, carry):
+        i = index // (SPECTRA // group)
+        t0 = (index % (SPECTRA // group)) * group
+        rows = pl.ds(pl.multiple_of(i * PITCH, 8), FIRST)
+        block = jnp.concatenate(
             [
-                jnp.dot(second_w[:, q * SECOND : (q + 1) * SECOND], onehot, preferred_element_type=jnp.float32)
-                for q in range(2)
+                jnp.concatenate([frames[part, t0 + n, rows, :] for part in range(2)], axis=0)
+                for n in range(group)
             ],
             axis=1,
         ).astype(jnp.bfloat16)
-        half = lax.broadcasted_iota(jnp.int32, (8, 128), 0) // SUBW
-        masks = [number_k == 2 * v + half for v in range(FIRST // 8)]
-        low = half == 0
-        group = GROUP
-
-        def one(index, carry):
-            i = index // (SPECTRA // group)
-            t0 = (index % (SPECTRA // group)) * group
-            rows = pl.ds(pl.multiple_of(i * PITCH, 8), FIRST)
-            block = jnp.concatenate(
-                [
-                    jnp.concatenate([frames[part, t0 + n, rows, :] for part in range(2)], axis=0)
-                    for n in range(group)
-                ],
-                axis=1,
-            ).astype(jnp.bfloat16)
-            first = jnp.dot(first_w[...], block, preferred_element_type=jnp.float32)
-            rotated = []
-            for n in range(group):
-                real = first[:FIRST, n * SECOND : (n + 1) * SECOND]
-                imag = first[FIRST:, n * SECOND : (n + 1) * SECOND]
-                cosine, sine = twid[0], twid[1]
-                rotated.append(
-                    jnp.concatenate([real * cosine + imag * sine, imag * cosine - real * sine], axis=1)
-                )
-            rotated = jnp.concatenate(rotated, axis=0).astype(jnp.bfloat16)
-            second = jnp.dot(rotated, chosen, preferred_element_type=jnp.float32)
-            for n in range(group):
-                folded = []
-                for q in range(2):
-                    total = jnp.zeros((8, 128), jnp.float32)
-                    for v in range(FIRST // 8):
-                        piece = second[n * FIRST + v * 8 : n * FIRST + v * 8 + 8, q * 128 : q * 128 + 128]
-                        total = jnp.where(masks[v], piece, total)
-                    folded.append(total + pltpu.roll(total, SUBW, 0))
-                picked[i, pl.ds(pl.multiple_of((t0 + n) * 8, 8), 8), :] = jnp.where(low, folded[0], folded[1])
-            return carry
-
-        lax.fori_loop(0, LOCAL * SPECTRA // group, one, 0, unroll=UNROLL)
-        for i in range(LOCAL):
-            turned[pl.ds(i, 128, stride=LOCAL), :] = picked[i].T * (flags[i // 2].astype(jnp.float32) * (1.0 / math.sqrt(NCH)))
-        values = turned[...].reshape(8, CAP, LOCAL, LANES).astype(jnp.bfloat16)
-        out[0] = values
-        out[1] = values
+        first = jnp.dot(first_w[...], block, preferred_element_type=jnp.float32)
+        rotated = []
+        for n in range(group):
+            real = first[:FIRST, n * SECOND : (n + 1) * SECOND]
+            imag = first[FIRST:, n * SECOND : (n + 1) * SECOND]
+            cosine, sine = twid[0], twid[1]
+            rotated.append(
+                jnp.concatenate([real * cosine + imag * sine, imag * cosine - real * sine], axis=1)
+            )
+        rotated = jnp.concatenate(rotated, axis=0).astype(jnp.bfloat16)
+        second = jnp.dot(rotated, chosen, preferred_element_type=jnp.float32)
+        for n in range(group):
+            folded = []
+            for q in range(2):
+                total = jnp.zeros((8, 128), jnp.float32)
+                for v in range(FIRST // 8):
+                    piece = second[n * FIRST + v * 8 : n * FIRST + v * 8 + 8, q * 128 : q * 128 + 128]
+                    total = jnp.where(masks[v], piece, total)
+                folded.append(total + pltpu.roll(total, SUBW, 0))
+            picked[i, pl.ds(pl.multiple_of((t0 + n) * 8, 8), 8), :] = jnp.where(low, folded[0], folded[1])
+        return carry
+
+    lax.fori_loop(0, LOCAL * SPECTRA // group, one, 0, unroll=UNROLL)
+    for i in range(LOCAL):
+        turned[pl.ds(i, 128, stride=LOCAL), :] = picked[i].T * (flags[i // 2].astype(jnp.float32) * (1.0 / math.sqrt(NCH)))
+    values = turned[...].reshape(8, CAP, LOCAL, LANES).astype(jnp.bfloat16)
+    out[0] = values
+    out[1] = values
 
 
 def channelize(voltages, filter_taps, station_flags, subband_lists):
@@ -152,26 +189,14 @@
     first_w = jnp.asarray(complex_block(cos1, sin1).T, jnp.bfloat16)
     second_w = jnp.asarray(complex_block(cos2, sin2), jnp.bfloat16)
     twid = jnp.asarray(np.stack(table(NCH, FIRST, SECOND)), jnp.float32)
-    steps = NCH // CHUNK
     volts = voltages.reshape(2, LOCAL, SEGMENTS, NCH).transpose(0, 2, 1, 3)
 
-    def whole(*shape):
-        return pl.BlockSpec(shape, lambda n: (0,) * len(shape))
-
-    hbm = pl.BlockSpec(memory_space=pltpu.HBM)
+    hbm = pl.BlockSpec(memory_space=pl.ANY)
+    vmem = pl.BlockSpec(memory_space=pltpu.VMEM)
     return pl.pallas_call(
         channelize_kernel,
-        grid=(steps,),
-        in_specs=[
-            pl.BlockSpec((2, SEGMENTS, LOCAL, CHUNK), lambda n: (0, 0, 0, n)),
-            pl.BlockSpec((TAPS, CHUNK), lambda n: (0, n)),
-            hbm,
-            hbm,
-            hbm,
-            whole(8, CAP),
-            pl.BlockSpec(memory_space=pltpu.SMEM),
-        ],
-        out_specs=whole(2, 8, CAP, LOCAL, LANES),
+        in_specs=[hbm] * 5 + [vmem, pl.BlockSpec(memory_space=pltpu.SMEM)],
+        out_specs=vmem,
         out_shape=jax.ShapeDtypeStruct((2, 8, CAP, LOCAL, LANES), jnp.bfloat16),
         scratch_shapes=[
             pltpu.VMEM((2, SPECTRA, LOCAL * PITCH, SECOND), jnp.float32),
@@ -180,7 +205,10 @@
             pltpu.VMEM((2 * FIRST, 2 * FIRST), jnp.bfloat16),
             pltpu.VMEM((2, FIRST, SECOND), jnp.float32),
             pltpu.VMEM((2 * SECOND, 2 * SECOND), jnp.bfloat16),
+            pltpu.VMEM((2, SEGMENTS, LOCAL, NCH), jnp.bfloat16),
+            pltpu.VMEM((TAPS, NCH), jnp.float32),
             pltpu.SemaphoreType.DMA((3,)),
+            pltpu.SemaphoreType.DMA((len(CHUNKS), 2)),
         ],
         compiler_params=pltpu.CompilerParams(vmem_limit_bytes=VMEM_ALL),
         name="channelize",

time: 60.6 us -> 59.2 us (0.977)
  Pallas kernels: 24.2 us -> 22.9 us
    pallas_call x1, Pallas kernels: 15.3 us -> 14 us  [channelize(): pl.pallas_call(channelize_kernel, in_specs=[hbm] * 5 + [vmem, pl.BlockSpe...]
where the time goes in v4:
time: 59.2 us; the launch traced here: 58.9 us
  Pallas kernels  22.9 us (39%)
  waiting for transfers between devices  19.2 us (32%)
  starting transfers between devices  15.8 us (27%)
  local copies, waits for them, and re-layouts  0.75 us (1%)
    pallas_call x1, Pallas kernels, channelize(): pl.pallas_call(channelize_kernel, in_specs=[hbm] * 5 + [vmem, pl.BlockSpe...  14 us
    all_to_all x1, waiting for transfers between devices, per_device(): lax.all_to_all(selected, ('stn', 'chan'), 0, 0, axis_index_groups=members...  9.94 us
    ppermute x7, waiting for transfers between devices, exchange(): return lax.ppermute(array, 'stn', [(i, i ^ flip) for i in range(16)])  9.22 us
    pallas_call x2, Pallas kernels, correlate(): pl.pallas_call(functools.partial(correlate_kernel, count), in_specs=specs...  8.89 us
    ppermute x7, starting transfers between devices, exchange(): return lax.ppermute(array, 'stn', [(i, i ^ flip) for i in range(16)])  8.2 us
    all_to_all x1, starting transfers between devices, per_device(): lax.all_to_all(selected, ('stn', 'chan'), 0, 0, axis_index_groups=members...  7.6 us
  transfers between devices with their start and end apart: 8, of which 7 were waited for; matrix products, arithmetic and copies ran while one was open for 0% of the time, Pallas kernels for 6%

profile of v4, /device:TPU:1, one launch (start us, length us, event | category | flops | bytes accessed | tf_op | source)
XLA Modules:
  0.0 58.9 jit_solution(5258568062534642041)
XLA Ops:
  0.0 14.0 %channelize.1 = bf16[2,8,16,8,128]{4,3,2,1,0:T(8,128)(2,1)} custom-call(bf16[2,31,8,8192]{3,2,1,0:T(8,128)(2,1)} %bitcast.20, f32[16,8192]{1,0:T(8,128)} %refs_1_.3, bf16[128,128]{1,0:T(8,128)(2,1)} %constant.91.clone.refs_2_, f32[2,64,128]{2,1,0:T(8,128)} %constant.93.clone.refs_3_, bf16[256,256]{1,0:T(8,128)(2,1)} %constant.92.clone.refs_4_, ...), custom_call_target="tpu_custom_call" | custom-call | tf_op jit(solution)/shard_map/channelize/pallas_call | solution.py:196
  14.0 7.6 %all-to-all-start = ((bf16[16,16,8,128]{3,2,1,0:T(8,128)(2,1)}), bf16[16,16,8,128]{3,2,1,0:T(8,128)(2,1)S(1)}, u32[]{:S(2)}, u32[]{:S(2)}) async-start(bf16[16,16,8,128]{3,2,1,0:T(8,128)(2,1)} %bitcast.21), calls=%async_computation | async-start | bytes 1048576 | tf_op jit(solution)/shard_map/all_to_all | solution.py:300
  21.7 9.9 %all-to-all-done = bf16[16,16,8,128]{3,2,1,0:T(8,128)(2,1)S(1)} async-done(((bf16[16,16,8,128]{3,2,1,0:T(8,128)(2,1)}), bf16[16,16,8,128]{3,2,1,0:T(8,128)(2,1)S(1)}, u32[]{:S(2)}, u32[]{:S(2)}) %all-to-all-start) | async-done | bytes 524320 | tf_op jit(solution)/shard_map/all_to_all | solution.py:300
  31.6 0.1 broadcast_select_fusion
  31.7 2.5 %collective-permute-start.3 = (bf16[8,16,8,128]{3,2,1,0:T(8,128)(2,1)S(1)}, bf16[8,16,8,128]{3,2,1,0:T(8,128)(2,1)S(1)}, u32[]{:S(2)}, u32[]{:S(2)}) collective-permute-start(bf16[8,16,8,128]{3,2,1,0:T(8,128)(2,1)S(1)} %get-tuple-element.13), channel_id=1, source_target_pairs={{0,8},{8,0},{16,24},{24,16},{32,40},{40,32},{48,56},{56,48},{64,72... | collective-permute-start | bytes 786440 | tf_op jit(solution)/shard_map/ppermute | solution.py:307
  34.2 0.1 broadcast_select_fusion.1
  34.2 3.7 %collective-permute-start.2 = (bf16[8,16,8,128]{3,2,1,0:T(8,128)(2,1)S(1)}, bf16[8,16,8,128]{3,2,1,0:T(8,128)(2,1)S(1)}, u32[]{:S(2)}, u32[]{:S(2)}) collective-permute-start(bf16[8,16,8,128]{3,2,1,0:T(8,128)(2,1)S(1)} %get-tuple-element.16), channel_id=1, source_target_pairs={{0,32},{8,40},{16,48},{24,56},{32,0},{40,8},{48,16},{56,24},{64,96... | collective-permute-start | bytes 786440 | tf_op jit(solution)/shard_map/ppermute | solution.py:307
  37.9 0.4 collective-permute-start.1
  38.3 0.3 collective-permute-start
  38.6 0.1 pad_add_fusion.refs_0_
  38.7 0.0 collective-permute-done.3.refs_5_
  38.7 0.7 %copy-done = s32[8]{0:T(128)S(1)} copy-done((s32[8]{0:T(128)S(1)}, s32[8]{0:T(128)}, u32[]{:S(2)}) %copy-start) | copy-done | bytes 56
  39.4 3.5 %correlate.2.refs_9_ = f32[9,64,64,128]{3,2,1,0:T(8,128)} custom-call(s32[4]{0:T(128)S(1)} %pad_add_fusion.refs_0_, s32[8]{0:T(128)S(1)} %copy-done, bf16[8,16,8,128]{3,2,1,0:T(8,128)(2,1)S(1)} %get-tuple-element.15.refs_2_.refs_3_, bf16[8,16,8,128]{3,2,1,0:T(8,128)(2,1)S(1)} %get-tuple-element.15.refs_2_.refs_3_, ...), custom_call_target="tpu_custom_call" | custom-call | tf_op jit(solution)/shard_map/correlate/pallas_call | solution.py:275
  42.9 1.8 %collective-permute-done.2.refs_7_ = bf16[8,16,8,128]{3,2,1,0:T(8,128)(2,1)S(1)} collective-permute-done((bf16[8,16,8,128]{3,2,1,0:T(8,128)(2,1)S(1)}, bf16[8,16,8,128]{3,2,1,0:T(8,128)(2,1)S(1)}, u32[]{:S(2)}, u32[]{:S(2)}) %collective-permute-start.2) | collective-permute-done | bytes 262176 | tf_op jit(solution)/shard_map/ppermute | solution.py:307
  44.6 5.7 %collective-permute-done.1.refs_5_ = bf16[8,16,8,128]{3,2,1,0:T(8,128)(2,1)S(1)} collective-permute-done((bf16[8,16,8,128]{3,2,1,0:T(8,128)(2,1)S(1)}, bf16[8,16,8,128]{3,2,1,0:T(8,128)(2,1)S(1)}, u32[]{:S(2)}, u32[]{:S(2)}) %collective-permute-start.1) | collective-permute-done | bytes 262176 | tf_op jit(solution)/shard_map/ppermute | solution.py:307
  50.3 0.4 collective-permute-done.refs_3_
  50.8 0.8 %collective-permute-start.4 = (bf16[8,16,8,128]{3,2,1,0:T(8,128)(2,1)S(1)}, bf16[8,16,8,128]{3,2,1,0:T(8,128)(2,1)S(1)}, u32[]{:S(2)}, u32[]{:S(2)}) collective-permute-start(bf16[8,16,8,128]{3,2,1,0:T(8,128)(2,1)S(1)} %collective-permute-done.refs_3_), channel_id=1, source_target_pairs={{0,8},{8,0},{16,24},{24,16},{32,40},{40,32},{48,56},{56,48},{64,72... | collective-permute-start | bytes 786440 | tf_op jit(solution)/shard_map/ppermute | solution.py:307
  51.6 0.0 collective-permute-start.5
  51.6 0.5 collective-permute-start.6
  52.1 0.1 stack.38.refs_0_
  52.2 0.6 collective-permute-done.4.refs_4_
  52.7 0.4 collective-permute-done.5.refs_6_
  53.1 0.4 collective-permute-done.6.refs_8_
  53.5 5.4 %correlate.3 = f32[9,64,64,128]{3,2,1,0:T(8,128)} custom-call(s32[7]{0:T(128)S(1)} %stack.38.refs_0_, s32[8]{0:T(128)S(1)} %copy-done.1, bf16[8,16,8,128]{3,2,1,0:T(8,128)(2,1)S(1)} %get-tuple-element.15.refs_2_.refs_3_, bf16[8,16,8,128]{3,2,1,0:T(8,128)(2,1)S(1)} %collective-permute-done.refs_3_, ...), custom_call_target="tpu_custom_call", output_to_operand_aliasing={{}: (9, {})} | custom-call | tf_op jit(solution)/shard_map/correlate/pallas_call | solution.py:275
  (3 shorter events, 0.0 us)
Async XLA Ops:
  0.0 53.5 %copy-start.1 = (s32[8]{0:T(128)S(1)}, s32[8]{0:T(128)}, u32[]{:S(2)}) copy-start(s32[8]{0:T(128)} %refs_1_.5) | copy-start | bytes 100
  14.0 17.6 %all-to-all-start = ((bf16[16,16,8,128]{3,2,1,0:T(8,128)(2,1)}), bf16[16,16,8,128]{3,2,1,0:T(8,128)(2,1)S(1)}, u32[]{:S(2)}, u32[]{:S(2)}) async-start(bf16[16,16,8,128]{3,2,1,0:T(8,128)(2,1)} %bitcast.21), calls=%async_computation | async-start | bytes 1048576 | tf_op jit(solution)/shard_map/all_to_all | solution.py:300
  31.7 7.0 %collective-permute-start.3 = (bf16[8,16,8,128]{3,2,1,0:T(8,128)(2,1)S(1)}, bf16[8,16,8,128]{3,2,1,0:T(8,128)(2,1)S(1)}, u32[]{:S(2)}, u32[]{:S(2)}) collective-permute-start(bf16[8,16,8,128]{3,2,1,0:T(8,128)(2,1)S(1)} %get-tuple-element.13), channel_id=1, source_target_pairs={{0,8},{8,0},{16,24},{24,16},{32,40},{40,32},{48,56},{56,48},{64,72... | collective-permute-start | bytes 786440 | tf_op jit(solution)/shard_map/ppermute | solution.py:307
  34.2 10.4 %collective-permute-start.2 = (bf16[8,16,8,128]{3,2,1,0:T(8,128)(2,1)S(1)}, bf16[8,16,8,128]{3,2,1,0:T(8,128)(2,1)S(1)}, u32[]{:S(2)}, u32[]{:S(2)}) collective-permute-start(bf16[8,16,8,128]{3,2,1,0:T(8,128)(2,1)S(1)} %get-tuple-element.16), channel_id=1, source_target_pairs={{0,32},{8,40},{16,48},{24,56},{32,0},{40,8},{48,16},{56,24},{64,96... | collective-permute-start | bytes 786440 | tf_op jit(solution)/shard_map/ppermute | solution.py:307
  37.9 12.4 %collective-permute-start.1 = (bf16[8,16,8,128]{3,2,1,0:T(8,128)(2,1)S(1)}, bf16[8,16,8,128]{3,2,1,0:T(8,128)(2,1)S(1)}, u32[]{:S(2)}, u32[]{:S(2)}) collective-permute-start(bf16[8,16,8,128]{3,2,1,0:T(8,128)(2,1)S(1)} %get-tuple-element.17), channel_id=1, source_target_pairs={{0,48},{8,56},{16,32},{24,40},{32,16},{40,24},{48,0},{56,8},{64,11... | collective-permute-start | bytes 786440 | tf_op jit(solution)/shard_map/ppermute | solution.py:307
  38.3 12.4 %collective-permute-start = (bf16[8,16,8,128]{3,2,1,0:T(8,128)(2,1)S(1)}, bf16[8,16,8,128]{3,2,1,0:T(8,128)(2,1)S(1)}, u32[]{:S(2)}, u32[]{:S(2)}) collective-permute-start(bf16[8,16,8,128]{3,2,1,0:T(8,128)(2,1)S(1)} %get-tuple-element.18), channel_id=1, source_target_pairs={{0,16},{8,24},{16,0},{24,8},{32,48},{40,56},{48,32},{56,40},{64,80... | collective-permute-start | bytes 786440 | tf_op jit(solution)/shard_map/ppermute | solution.py:307
  38.7 0.7 %copy-start = (s32[8]{0:T(128)S(1)}, s32[8]{0:T(128)}, u32[]{:S(2)}) copy-start(s32[8]{0:T(128)} %refs_1_.5) | copy-start | bytes 100
  50.8 2.0 %collective-permute-start.4 = (bf16[8,16,8,128]{3,2,1,0:T(8,128)(2,1)S(1)}, bf16[8,16,8,128]{3,2,1,0:T(8,128)(2,1)S(1)}, u32[]{:S(2)}, u32[]{:S(2)}) collective-permute-start(bf16[8,16,8,128]{3,2,1,0:T(8,128)(2,1)S(1)} %collective-permute-done.refs_3_), channel_id=1, source_target_pairs={{0,8},{8,0},{16,24},{24,16},{32,40},{40,32},{48,56},{56,48},{64,72... | collective-permute-start | bytes 786440 | tf_op jit(solution)/shard_map/ppermute | solution.py:307
  51.6 1.5 %collective-permute-start.5 = (bf16[8,16,8,128]{3,2,1,0:T(8,128)(2,1)S(1)}, bf16[8,16,8,128]{3,2,1,0:T(8,128)(2,1)S(1)}, u32[]{:S(2)}, u32[]{:S(2)}) collective-permute-start(bf16[8,16,8,128]{3,2,1,0:T(8,128)(2,1)S(1)} %collective-permute-done.1.refs_5_), channel_id=1, source_target_pairs={{0,8},{8,0},{16,24},{24,16},{32,40},{40,32},{48,56},{56,48},{64,72... | collective-permute-start | bytes 786440 | tf_op jit(solution)/shard_map/ppermute | solution.py:307
  51.6 1.9 %collective-permute-start.6 = (bf16[8,16,8,128]{3,2,1,0:T(8,128)(2,1)S(1)}, bf16[8,16,8,128]{3,2,1,0:T(8,128)(2,1)S(1)}, u32[]{:S(2)}, u32[]{:S(2)}) collective-permute-start(bf16[8,16,8,128]{3,2,1,0:T(8,128)(2,1)S(1)} %collective-permute-done.2.refs_7_), channel_id=1, source_target_pairs={{0,8},{8,0},{16,24},{24,16},{32,40},{40,32},{48,56},{56,48},{64,72... | collective-permute-start | bytes 786440 | tf_op jit(solution)/shard_map/ppermute | solution.py:307

commit v5 on v4

--- a/solution.py
+++ b/solution.py
@@ -46,26 +46,31 @@
     return split_taps(low), split_taps(high), split_taps([a + b for a, b in zip(low, high)])
 
 
-def sliding(tree, values, start=None):
-    length = (len(values) + 1) // 2
+def remembered(function):
+    return functools.lru_cache(maxsize=None)(function)
+
+
+def sliding(tree, length, value, emit, start=None):
     if isinstance(tree, list):
-        totals = []
-        for t in range(length):
-            total = None if start is None else start[t]
+        totals = dict(enumerate(start or ()))
+        for n in range(2 * length - 1):
             for j in range(length):
-                term = tree[j] * values[t + j]
-                total = term if total is None else total + term
-            totals.append(total)
-        return totals
+                t = n - j
+                if 0 <= t < length:
+                    term = tree[j] * value(n)
+                    totals[t] = totals[t] + term if t in totals else term
+            if n >= length - 1:
+                emit(n - length + 1, totals.pop(n - length + 1))
+        return
     low, high, both = tree
     half = length // 2
-    span = range(length - 1)
-    shared = sliding(both, values[half : half + length - 1])
+    shared = [None] * half
+    sliding(both, half, lambda n: value(n + half), shared.__setitem__)
     first = shared if start is None else [a + b for a, b in zip(start[:half], shared)]
+    sliding(low, half, remembered(lambda n: value(n) - value(n + half)), emit, first)
     second = shared if start is None else [a + b for a, b in zip(start[half:], shared)]
-    return sliding(low, [values[n] - values[n + half] for n in span], first) + sliding(
-        high, [values[n + length] - values[n + half] for n in span], second
-    )
+    late = remembered(lambda n: value(n + length) - value(n + half))
+    sliding(high, half, late, lambda t, total: emit(t + half, total), second)
 
 
 def channelize_kernel(*refs):
@@ -102,9 +107,12 @@
         coeffs = [jnp.broadcast_to(taps[j : j + 1, lanes], (LOCAL, SECOND)) for j in range(TAPS)]
         tree = split_taps(coeffs)
         for part in range(2):
-            values = [volts[part, seg, :, lanes].astype(jnp.float32) for seg in range(SEGMENTS)]
-            for t, total in enumerate(sliding(tree, values)):
+            value = lambda seg: volts[part, seg, :, lanes].astype(jnp.float32)
+
+            def store(t, total):
                 frames[part, t, pl.ds(row, LOCAL, stride=PITCH), :] = total
+
+            sliding(tree, TAPS, value, store)
         return carry
 
     for n in range(len(CHUNKS)):
@@ -318,9 +326,11 @@
     ahead = {flip: 2 * ((col ^ flip) - col + 4) % 8 for flip in (1, 2, 3)}
     join = functools.partial(correlate, group=group, counts=subband_counts, own=own)
     total = join(None, pairs=[(0 * core, own), (0 * core + 8, far), (1 + 6 * core, spare)])
-    *arrived, total = lax.optimization_barrier((*(moved[flip] for flip in (1, 3, 2)), total))
-    pairs = []
-    for flip, block in zip((1, 3, 2), arrived):
+    far_block, after = lax.optimization_barrier((moved[2], total))
+    total = join(after, pairs=[(ahead[2], far_block)])
+    *near, total = lax.optimization_barrier((moved[1], moved[3], total))
+    pairs = [(ahead[2] + side, exchange(far_block, 1))]
+    for flip, block in zip((1, 3), near):
         pairs += [(ahead[flip], block), (ahead[flip] + side, exchange(block, 1))]
     total = join(total, pairs=pairs)
     return total[None]

time: 59.2 us -> 58.5 us (0.988)
  waiting for transfers between devices: 19.2 us -> 16.3 us
  Pallas kernels: 22.9 us -> 25 us
    ppermute x7, waiting for transfers between devices: 9.22 us -> 6.32 us  [exchange(): return lax.ppermute(array, 'stn', [(i, i ^ flip) for i in range(16)])]
    pallas_call x2 -> x3, Pallas kernels: 8.89 us -> 11 us  [correlate(): pl.pallas_call(functools.partial(correlate_kernel, count), in_specs=specs...]
  transfers between devices with their start and end apart: 8 -> 8, of which waited for: 7 -> 7; matrix products, arithmetic and copies ran while one was open for 0% -> 0% of each run, Pallas kernels for 6% -> 11%
where the time goes in v5:
time: 58.5 us; the launch traced here: 58.2 us
  Pallas kernels  25 us (43%)
  waiting for transfers between devices  16.3 us (28%)
  starting transfers between devices  15.8 us (27%)
  local copies, waits for them, and re-layouts  0.75 us (1%)
    pallas_call x1, Pallas kernels, channelize(): pl.pallas_call(channelize_kernel, in_specs=[hbm] * 5 + [vmem, pl.BlockSpe...  14 us
    pallas_call x3, Pallas kernels, correlate(): pl.pallas_call(functools.partial(correlate_kernel, count), in_specs=specs...  11 us
    all_to_all x1, waiting for transfers between devices, per_device(): lax.all_to_all(selected, ('stn', 'chan'), 0, 0, axis_index_groups=members...  9.94 us
    ppermute x7, starting transfers between devices, exchange(): return lax.ppermute(array, 'stn', [(i, i ^ flip) for i in range(16)])  8.21 us
    all_to_all x1, starting transfers between devices, per_device(): lax.all_to_all(selected, ('stn', 'chan'), 0, 0, axis_index_groups=members...  7.59 us
    ppermute x7, waiting for transfers between devices, exchange(): return lax.ppermute(array, 'stn', [(i, i ^ flip) for i in range(16)])  6.32 us
  transfers between devices with their start and end apart: 8, of which 7 were waited for; matrix products, arithmetic and copies ran while one was open for 0% of the time, Pallas kernels for 11%

profile of v5, /device:TPU:1, one launch (start us, length us, event | category | flops | bytes accessed | tf_op | source)
XLA Modules:
  0.0 58.2 jit_solution(9644137528751237404)
XLA Ops:
  0.0 14.0 %channelize.1 = bf16[2,8,16,8,128]{4,3,2,1,0:T(8,128)(2,1)} custom-call(bf16[2,31,8,8192]{3,2,1,0:T(8,128)(2,1)} %bitcast.20, f32[16,8192]{1,0:T(8,128)} %refs_1_.4, bf16[128,128]{1,0:T(8,128)(2,1)} %constant.91.clone.refs_2_, f32[2,64,128]{2,1,0:T(8,128)} %constant.93.clone.refs_3_, bf16[256,256]{1,0:T(8,128)(2,1)} %constant.92.clone.refs_4_, ...), custom_call_target="tpu_custom_call" | custom-call | tf_op jit(solution)/shard_map/channelize/pallas_call | solution.py:204
  14.0 7.6 %all-to-all-start = ((bf16[16,16,8,128]{3,2,1,0:T(8,128)(2,1)}), bf16[16,16,8,128]{3,2,1,0:T(8,128)(2,1)S(1)}, u32[]{:S(2)}, u32[]{:S(2)}) async-start(bf16[16,16,8,128]{3,2,1,0:T(8,128)(2,1)} %bitcast.21), calls=%async_computation | async-start | bytes 1048576 | tf_op jit(solution)/shard_map/all_to_all | solution.py:308
  21.7 9.9 %all-to-all-done = bf16[16,16,8,128]{3,2,1,0:T(8,128)(2,1)S(1)} async-done(((bf16[16,16,8,128]{3,2,1,0:T(8,128)(2,1)}), bf16[16,16,8,128]{3,2,1,0:T(8,128)(2,1)S(1)}, u32[]{:S(2)}, u32[]{:S(2)}) %all-to-all-start) | async-done | bytes 524320 | tf_op jit(solution)/shard_map/all_to_all | solution.py:308
  31.6 0.1 broadcast_select_fusion
  31.7 0.1 broadcast_select_fusion.1
  31.8 2.5 %collective-permute-start.1 = (bf16[8,16,8,128]{3,2,1,0:T(8,128)(2,1)S(1)}, bf16[8,16,8,128]{3,2,1,0:T(8,128)(2,1)S(1)}, u32[]{:S(2)}, u32[]{:S(2)}) collective-permute-start(bf16[8,16,8,128]{3,2,1,0:T(8,128)(2,1)S(1)} %get-tuple-element.19), channel_id=1, source_target_pairs={{0,8},{8,0},{16,24},{24,16},{32,40},{40,32},{48,56},{56,48},{64,72... | collective-permute-start | bytes 786440 | tf_op jit(solution)/shard_map/ppermute | solution.py:315
  34.2 3.6 %collective-permute-start = (bf16[8,16,8,128]{3,2,1,0:T(8,128)(2,1)S(1)}, bf16[8,16,8,128]{3,2,1,0:T(8,128)(2,1)S(1)}, u32[]{:S(2)}, u32[]{:S(2)}) collective-permute-start(bf16[8,16,8,128]{3,2,1,0:T(8,128)(2,1)S(1)} %get-tuple-element.20), channel_id=1, source_target_pairs={{0,32},{8,40},{16,48},{24,56},{32,0},{40,8},{48,16},{56,24},{64,96... | collective-permute-start | bytes 786440 | tf_op jit(solution)/shard_map/ppermute | solution.py:315
  37.8 0.4 collective-permute-start.4
  38.3 0.3 collective-permute-start.3
  38.6 0.1 pad_add_fusion.1.refs_0_
  38.7 0.1 pad_add_fusion.refs_0_
  38.7 0.7 %copy-done = s32[8]{0:T(128)S(1)} copy-done((s32[8]{0:T(128)S(1)}, s32[8]{0:T(128)}, u32[]{:S(2)}) %copy-start) | copy-done | bytes 56
  39.4 3.5 %correlate.3.refs_4_ = f32[9,64,64,128]{3,2,1,0:T(8,128)} custom-call(s32[4]{0:T(128)S(1)} %pad_add_fusion.refs_0_, s32[8]{0:T(128)S(1)} %copy-done, bf16[8,16,8,128]{3,2,1,0:T(8,128)(2,1)S(1)} %get-tuple-element.17.refs_2_.refs_3_, bf16[8,16,8,128]{3,2,1,0:T(8,128)(2,1)S(1)} %get-tuple-element.17.refs_2_.refs_3_, ...), custom_call_target="tpu_custom_call" | custom-call | tf_op jit(solution)/shard_map/correlate/pallas_call | solution.py:283
  42.9 1.6 %collective-permute-done.refs_3_ = bf16[8,16,8,128]{3,2,1,0:T(8,128)(2,1)S(1)} collective-permute-done((bf16[8,16,8,128]{3,2,1,0:T(8,128)(2,1)S(1)}, bf16[8,16,8,128]{3,2,1,0:T(8,128)(2,1)S(1)}, u32[]{:S(2)}, u32[]{:S(2)}) %collective-permute-start) | collective-permute-done | bytes 262176 | tf_op jit(solution)/shard_map/ppermute | solution.py:315
  44.5 2.7 %correlate.4.refs_8_ = f32[9,64,64,128]{3,2,1,0:T(8,128)} custom-call(s32[2]{0:T(128)S(1)} %pad_add_fusion.1.refs_0_, s32[8]{0:T(128)S(1)} %copy-done, bf16[8,16,8,128]{3,2,1,0:T(8,128)(2,1)S(1)} %get-tuple-element.17.refs_2_.refs_3_, bf16[8,16,8,128]{3,2,1,0:T(8,128)(2,1)S(1)} %collective-permute-done.refs_3_, ...), custom_call_target="tpu_custom_call", output_to_operand_aliasing={{}: (4, {})} | custom-call | tf_op jit(solution)/shard_map/correlate/pallas_call | solution.py:283
  47.2 3.0 %collective-permute-done.4.refs_6_ = bf16[8,16,8,128]{3,2,1,0:T(8,128)(2,1)S(1)} collective-permute-done((bf16[8,16,8,128]{3,2,1,0:T(8,128)(2,1)S(1)}, bf16[8,16,8,128]{3,2,1,0:T(8,128)(2,1)S(1)}, u32[]{:S(2)}, u32[]{:S(2)}) %collective-permute-start.4) | collective-permute-done | bytes 262176 | tf_op jit(solution)/shard_map/ppermute | solution.py:315
  50.2 0.4 collective-permute-done.3.refs_4_
  50.6 0.9 %collective-permute-start.5 = (bf16[8,16,8,128]{3,2,1,0:T(8,128)(2,1)S(1)}, bf16[8,16,8,128]{3,2,1,0:T(8,128)(2,1)S(1)}, u32[]{:S(2)}, u32[]{:S(2)}) collective-permute-start(bf16[8,16,8,128]{3,2,1,0:T(8,128)(2,1)S(1)} %collective-permute-done.3.refs_4_), channel_id=1, source_target_pairs={{0,8},{8,0},{16,24},{24,16},{32,40},{40,32},{48,56},{56,48},{64,72... | collective-permute-start | bytes 786440 | tf_op jit(solution)/shard_map/ppermute | solution.py:315
  51.5 0.5 collective-permute-start.2
  52.0 0.1 stack.41.refs_0_
  52.1 0.6 collective-permute-done.5.refs_5_
  52.7 0.4 collective-permute-done.6.refs_7_
  53.0 0.4 collective-permute-done.2.refs_3_
  53.4 4.8 %correlate.5 = f32[9,64,64,128]{3,2,1,0:T(8,128)} custom-call(s32[6]{0:T(128)S(1)} %stack.41.refs_0_, s32[8]{0:T(128)S(1)} %copy-done.1, bf16[8,16,8,128]{3,2,1,0:T(8,128)(2,1)S(1)} %get-tuple-element.17.refs_2_.refs_3_, bf16[8,16,8,128]{3,2,1,0:T(8,128)(2,1)S(1)} %collective-permute-done.2.refs_3_, ...), custom_call_target="tpu_custom_call", output_to_operand_aliasing={{}: (8, {})} | custom-call | tf_op jit(solution)/shard_map/correlate/pallas_call | solution.py:283
  (5 shorter events, 0.0 us)
Async XLA Ops:
  14.0 17.6 %all-to-all-start = ((bf16[16,16,8,128]{3,2,1,0:T(8,128)(2,1)}), bf16[16,16,8,128]{3,2,1,0:T(8,128)(2,1)S(1)}, u32[]{:S(2)}, u32[]{:S(2)}) async-start(bf16[16,16,8,128]{3,2,1,0:T(8,128)(2,1)} %bitcast.21), calls=%async_computation | async-start | bytes 1048576 | tf_op jit(solution)/shard_map/all_to_all | solution.py:308
  31.8 7.0 %collective-permute-start.1 = (bf16[8,16,8,128]{3,2,1,0:T(8,128)(2,1)S(1)}, bf16[8,16,8,128]{3,2,1,0:T(8,128)(2,1)S(1)}, u32[]{:S(2)}, u32[]{:S(2)}) collective-permute-start(bf16[8,16,8,128]{3,2,1,0:T(8,128)(2,1)S(1)} %get-tuple-element.19), channel_id=1, source_target_pairs={{0,8},{8,0},{16,24},{24,16},{32,40},{40,32},{48,56},{56,48},{64,72... | collective-permute-start | bytes 786440 | tf_op jit(solution)/shard_map/ppermute | solution.py:315
  34.2 10.2 %collective-permute-start = (bf16[8,16,8,128]{3,2,1,0:T(8,128)(2,1)S(1)}, bf16[8,16,8,128]{3,2,1,0:T(8,128)(2,1)S(1)}, u32[]{:S(2)}, u32[]{:S(2)}) collective-permute-start(bf16[8,16,8,128]{3,2,1,0:T(8,128)(2,1)S(1)} %get-tuple-element.20), channel_id=1, source_target_pairs={{0,32},{8,40},{16,48},{24,56},{32,0},{40,8},{48,16},{56,24},{64,96... | collective-permute-start | bytes 786440 | tf_op jit(solution)/shard_map/ppermute | solution.py:315
  37.8 12.4 %collective-permute-start.4 = (bf16[8,16,8,128]{3,2,1,0:T(8,128)(2,1)S(1)}, bf16[8,16,8,128]{3,2,1,0:T(8,128)(2,1)S(1)}, u32[]{:S(2)}, u32[]{:S(2)}) collective-permute-start(bf16[8,16,8,128]{3,2,1,0:T(8,128)(2,1)S(1)} %get-tuple-element.15), channel_id=1, source_target_pairs={{0,48},{8,56},{16,32},{24,40},{32,16},{40,24},{48,0},{56,8},{64,11... | collective-permute-start | bytes 786440 | tf_op jit(solution)/shard_map/ppermute | solution.py:315
  38.3 12.3 %collective-permute-start.3 = (bf16[8,16,8,128]{3,2,1,0:T(8,128)(2,1)S(1)}, bf16[8,16,8,128]{3,2,1,0:T(8,128)(2,1)S(1)}, u32[]{:S(2)}, u32[]{:S(2)}) collective-permute-start(bf16[8,16,8,128]{3,2,1,0:T(8,128)(2,1)S(1)} %get-tuple-element.18), channel_id=1, source_target_pairs={{0,16},{8,24},{16,0},{24,8},{32,48},{40,56},{48,32},{56,40},{64,80... | collective-permute-start | bytes 786440 | tf_op jit(solution)/shard_map/ppermute | solution.py:315
  38.7 0.7 %copy-start = (s32[8]{0:T(128)S(1)}, s32[8]{0:T(128)}, u32[]{:S(2)}) copy-start(s32[8]{0:T(128)} %refs_1_.7) | copy-start | bytes 100
  42.9 10.6 %copy-start.1 = (s32[8]{0:T(128)S(1)}, s32[8]{0:T(128)}, u32[]{:S(2)}) copy-start(s32[8]{0:T(128)} %refs_1_.7) | copy-start | bytes 100
  50.6 2.0 %collective-permute-start.5 = (bf16[8,16,8,128]{3,2,1,0:T(8,128)(2,1)S(1)}, bf16[8,16,8,128]{3,2,1,0:T(8,128)(2,1)S(1)}, u32[]{:S(2)}, u32[]{:S(2)}) collective-permute-start(bf16[8,16,8,128]{3,2,1,0:T(8,128)(2,1)S(1)} %collective-permute-done.3.refs_4_), channel_id=1, source_target_pairs={{0,8},{8,0},{16,24},{24,16},{32,40},{40,32},{48,56},{56,48},{64,72... | collective-permute-start | bytes 786440 | tf_op jit(solution)/shard_map/ppermute | solution.py:315
  51.5 1.5 %collective-permute-start.6 = (bf16[8,16,8,128]{3,2,1,0:T(8,128)(2,1)S(1)}, bf16[8,16,8,128]{3,2,1,0:T(8,128)(2,1)S(1)}, u32[]{:S(2)}, u32[]{:S(2)}) collective-permute-start(bf16[8,16,8,128]{3,2,1,0:T(8,128)(2,1)S(1)} %collective-permute-done.4.refs_6_), channel_id=1, source_target_pairs={{0,8},{8,0},{16,24},{24,16},{32,40},{40,32},{48,56},{56,48},{64,72... | collective-permute-start | bytes 786440 | tf_op jit(solution)/shard_map/ppermute | solution.py:315
  51.5 1.9 %collective-permute-start.2 = (bf16[8,16,8,128]{3,2,1,0:T(8,128)(2,1)S(1)}, bf16[8,16,8,128]{3,2,1,0:T(8,128)(2,1)S(1)}, u32[]{:S(2)}, u32[]{:S(2)}) collective-permute-start(bf16[8,16,8,128]{3,2,1,0:T(8,128)(2,1)S(1)} %collective-permute-done.refs_3_), channel_id=1, source_target_pairs={{0,8},{8,0},{16,24},{24,16},{32,40},{40,32},{48,56},{56,48},{64,72... | collective-permute-start | bytes 786440 | tf_op jit(solution)/shard_map/ppermute | solution.py:315

commit v6 on v5

--- a/solution.py
+++ b/solution.py
@@ -23,7 +23,7 @@
 FUNROLL = 2
 DIRECT = 4
 PITCH = FIRST + 8
-GROUP = 8
+GROUP = 16
 UNROLL = 8
 VMEM = 48 * 1024 * 1024
 VMEM_ALL = 60 * 1024 * 1024

time: 58.5 us -> 57.7 us (0.986)
  Pallas kernels: 25 us -> 24.2 us
    pallas_call x1, Pallas kernels: 14 us -> 13.2 us  [channelize(): pl.pallas_call(channelize_kernel, in_specs=[hbm] * 5 + [vmem, pl.BlockSpe...]
where the time goes in v6:
time: 57.7 us; the launch traced here: 57.4 us
  Pallas kernels  24.2 us (42%)
  waiting for transfers between devices  16.3 us (28%)
  starting transfers between devices  15.8 us (27%)
  local copies, waits for them, and re-layouts  0.75 us (1%)
    pallas_call x1, Pallas kernels, channelize(): pl.pallas_call(channelize_kernel, in_specs=[hbm] * 5 + [vmem, pl.BlockSpe...  13.2 us
    pallas_call x3, Pallas kernels, correlate(): pl.pallas_call(functools.partial(correlate_kernel, count), in_specs=specs...  11 us
    all_to_all x1, waiting for transfers between devices, per_device(): lax.all_to_all(selected, ('stn', 'chan'), 0, 0, axis_index_groups=members...  9.95 us
    ppermute x7, starting transfers between devices, exchange(): return lax.ppermute(array, 'stn', [(i, i ^ flip) for i in range(16)])  8.18 us
    all_to_all x1, starting transfers between devices, per_device(): lax.all_to_all(selected, ('stn', 'chan'), 0, 0, axis_index_groups=members...  7.61 us
    ppermute x7, waiting for transfers between devices, exchange(): return lax.ppermute(array, 'stn', [(i, i ^ flip) for i in range(16)])  6.33 us
  transfers between devices with their start and end apart: 8, of which 7 were waited for; matrix products, arithmetic and copies ran while one was open for 0% of the time, Pallas kernels for 11%

profile of v6, /device:TPU:1, one launch (start us, length us, event | category | flops | bytes accessed | tf_op | source)
XLA Modules:
  0.0 57.4 jit_solution(1262925106673729221)
XLA Ops:
  0.0 13.2 %channelize.1 = bf16[2,8,16,8,128]{4,3,2,1,0:T(8,128)(2,1)} custom-call(bf16[2,31,8,8192]{3,2,1,0:T(8,128)(2,1)} %bitcast.20, f32[16,8192]{1,0:T(8,128)} %refs_1_.4, bf16[128,128]{1,0:T(8,128)(2,1)} %constant.91.clone.refs_2_, f32[2,64,128]{2,1,0:T(8,128)} %constant.93.clone.refs_3_, bf16[256,256]{1,0:T(8,128)(2,1)} %constant.92.clone.refs_4_, ...), custom_call_target="tpu_custom_call" | custom-call | tf_op jit(solution)/shard_map/channelize/pallas_call | solution.py:204
  13.2 7.6 %all-to-all-start = ((bf16[16,16,8,128]{3,2,1,0:T(8,128)(2,1)}), bf16[16,16,8,128]{3,2,1,0:T(8,128)(2,1)S(1)}, u32[]{:S(2)}, u32[]{:S(2)}) async-start(bf16[16,16,8,128]{3,2,1,0:T(8,128)(2,1)} %bitcast.21), calls=%async_computation | async-start | bytes 1048576 | tf_op jit(solution)/shard_map/all_to_all | solution.py:308
  20.9 9.9 %all-to-all-done = bf16[16,16,8,128]{3,2,1,0:T(8,128)(2,1)S(1)} async-done(((bf16[16,16,8,128]{3,2,1,0:T(8,128)(2,1)}), bf16[16,16,8,128]{3,2,1,0:T(8,128)(2,1)S(1)}, u32[]{:S(2)}, u32[]{:S(2)}) %all-to-all-start) | async-done | bytes 524320 | tf_op jit(solution)/shard_map/all_to_all | solution.py:308
  30.9 0.1 broadcast_select_fusion
  30.9 0.1 broadcast_select_fusion.1
  31.0 2.5 %collective-permute-start.1 = (bf16[8,16,8,128]{3,2,1,0:T(8,128)(2,1)S(1)}, bf16[8,16,8,128]{3,2,1,0:T(8,128)(2,1)S(1)}, u32[]{:S(2)}, u32[]{:S(2)}) collective-permute-start(bf16[8,16,8,128]{3,2,1,0:T(8,128)(2,1)S(1)} %get-tuple-element.19), channel_id=1, source_target_pairs={{0,8},{8,0},{16,24},{24,16},{32,40},{40,32},{48,56},{56,48},{64,72... | collective-permute-start | bytes 786440 | tf_op jit(solution)/shard_map/ppermute | solution.py:315
  33.4 3.6 %collective-permute-start = (bf16[8,16,8,128]{3,2,1,0:T(8,128)(2,1)S(1)}, bf16[8,16,8,128]{3,2,1,0:T(8,128)(2,1)S(1)}, u32[]{:S(2)}, u32[]{:S(2)}) collective-permute-start(bf16[8,16,8,128]{3,2,1,0:T(8,128)(2,1)S(1)} %get-tuple-element.20), channel_id=1, source_target_pairs={{0,32},{8,40},{16,48},{24,56},{32,0},{40,8},{48,16},{56,24},{64,96... | collective-permute-start | bytes 786440 | tf_op jit(solution)/shard_map/ppermute | solution.py:315
  37.0 0.4 collective-permute-start.4
  37.5 0.3 collective-permute-start.3
  37.8 0.1 pad_add_fusion.1.refs_0_
  37.9 0.1 pad_add_fusion.refs_0_
  37.9 0.7 %copy-done = s32[8]{0:T(128)S(1)} copy-done((s32[8]{0:T(128)S(1)}, s32[8]{0:T(128)}, u32[]{:S(2)}) %copy-start) | copy-done | bytes 56
  38.6 3.5 %correlate.3.refs_4_ = f32[9,64,64,128]{3,2,1,0:T(8,128)} custom-call(s32[4]{0:T(128)S(1)} %pad_add_fusion.refs_0_, s32[8]{0:T(128)S(1)} %copy-done, bf16[8,16,8,128]{3,2,1,0:T(8,128)(2,1)S(1)} %get-tuple-element.17.refs_2_.refs_3_, bf16[8,16,8,128]{3,2,1,0:T(8,128)(2,1)S(1)} %get-tuple-element.17.refs_2_.refs_3_, ...), custom_call_target="tpu_custom_call" | custom-call | tf_op jit(solution)/shard_map/correlate/pallas_call | solution.py:283
  42.1 1.6 %collective-permute-done.refs_3_ = bf16[8,16,8,128]{3,2,1,0:T(8,128)(2,1)S(1)} collective-permute-done((bf16[8,16,8,128]{3,2,1,0:T(8,128)(2,1)S(1)}, bf16[8,16,8,128]{3,2,1,0:T(8,128)(2,1)S(1)}, u32[]{:S(2)}, u32[]{:S(2)}) %collective-permute-start) | collective-permute-done | bytes 262176 | tf_op jit(solution)/shard_map/ppermute | solution.py:315
  43.7 2.7 %correlate.4.refs_8_ = f32[9,64,64,128]{3,2,1,0:T(8,128)} custom-call(s32[2]{0:T(128)S(1)} %pad_add_fusion.1.refs_0_, s32[8]{0:T(128)S(1)} %copy-done, bf16[8,16,8,128]{3,2,1,0:T(8,128)(2,1)S(1)} %get-tuple-element.17.refs_2_.refs_3_, bf16[8,16,8,128]{3,2,1,0:T(8,128)(2,1)S(1)} %collective-permute-done.refs_3_, ...), custom_call_target="tpu_custom_call", output_to_operand_aliasing={{}: (4, {})} | custom-call | tf_op jit(solution)/shard_map/correlate/pallas_call | solution.py:283
  46.4 3.0 %collective-permute-done.4.refs_6_ = bf16[8,16,8,128]{3,2,1,0:T(8,128)(2,1)S(1)} collective-permute-done((bf16[8,16,8,128]{3,2,1,0:T(8,128)(2,1)S(1)}, bf16[8,16,8,128]{3,2,1,0:T(8,128)(2,1)S(1)}, u32[]{:S(2)}, u32[]{:S(2)}) %collective-permute-start.4) | collective-permute-done | bytes 262176 | tf_op jit(solution)/shard_map/ppermute | solution.py:315
  49.4 0.4 collective-permute-done.3.refs_4_
  49.8 0.9 %collective-permute-start.5 = (bf16[8,16,8,128]{3,2,1,0:T(8,128)(2,1)S(1)}, bf16[8,16,8,128]{3,2,1,0:T(8,128)(2,1)S(1)}, u32[]{:S(2)}, u32[]{:S(2)}) collective-permute-start(bf16[8,16,8,128]{3,2,1,0:T(8,128)(2,1)S(1)} %collective-permute-done.3.refs_4_), channel_id=1, source_target_pairs={{0,8},{8,0},{16,24},{24,16},{32,40},{40,32},{48,56},{56,48},{64,72... | collective-permute-start | bytes 786440 | tf_op jit(solution)/shard_map/ppermute | solution.py:315
  50.7 0.5 collective-permute-start.2
  51.2 0.1 stack.41.refs_0_
  51.3 0.6 collective-permute-done.5.refs_5_
  51.9 0.4 collective-permute-done.6.refs_7_
  52.2 0.4 collective-permute-done.2.refs_3_
  52.6 4.8 %correlate.5 = f32[9,64,64,128]{3,2,1,0:T(8,128)} custom-call(s32[6]{0:T(128)S(1)} %stack.41.refs_0_, s32[8]{0:T(128)S(1)} %copy-done.1, bf16[8,16,8,128]{3,2,1,0:T(8,128)(2,1)S(1)} %get-tuple-element.17.refs_2_.refs_3_, bf16[8,16,8,128]{3,2,1,0:T(8,128)(2,1)S(1)} %collective-permute-done.2.refs_3_, ...), custom_call_target="tpu_custom_call", output_to_operand_aliasing={{}: (8, {})} | custom-call | tf_op jit(solution)/shard_map/correlate/pallas_call | solution.py:283
  (5 shorter events, 0.0 us)
Async XLA Ops:
  13.2 17.6 %all-to-all-start = ((bf16[16,16,8,128]{3,2,1,0:T(8,128)(2,1)}), bf16[16,16,8,128]{3,2,1,0:T(8,128)(2,1)S(1)}, u32[]{:S(2)}, u32[]{:S(2)}) async-start(bf16[16,16,8,128]{3,2,1,0:T(8,128)(2,1)} %bitcast.21), calls=%async_computation | async-start | bytes 1048576 | tf_op jit(solution)/shard_map/all_to_all | solution.py:308
  31.0 7.0 %collective-permute-start.1 = (bf16[8,16,8,128]{3,2,1,0:T(8,128)(2,1)S(1)}, bf16[8,16,8,128]{3,2,1,0:T(8,128)(2,1)S(1)}, u32[]{:S(2)}, u32[]{:S(2)}) collective-permute-start(bf16[8,16,8,128]{3,2,1,0:T(8,128)(2,1)S(1)} %get-tuple-element.19), channel_id=1, source_target_pairs={{0,8},{8,0},{16,24},{24,16},{32,40},{40,32},{48,56},{56,48},{64,72... | collective-permute-start | bytes 786440 | tf_op jit(solution)/shard_map/ppermute | solution.py:315
  33.4 10.2 %collective-permute-start = (bf16[8,16,8,128]{3,2,1,0:T(8,128)(2,1)S(1)}, bf16[8,16,8,128]{3,2,1,0:T(8,128)(2,1)S(1)}, u32[]{:S(2)}, u32[]{:S(2)}) collective-permute-start(bf16[8,16,8,128]{3,2,1,0:T(8,128)(2,1)S(1)} %get-tuple-element.20), channel_id=1, source_target_pairs={{0,32},{8,40},{16,48},{24,56},{32,0},{40,8},{48,16},{56,24},{64,96... | collective-permute-start | bytes 786440 | tf_op jit(solution)/shard_map/ppermute | solution.py:315
  37.0 12.4 %collective-permute-start.4 = (bf16[8,16,8,128]{3,2,1,0:T(8,128)(2,1)S(1)}, bf16[8,16,8,128]{3,2,1,0:T(8,128)(2,1)S(1)}, u32[]{:S(2)}, u32[]{:S(2)}) collective-permute-start(bf16[8,16,8,128]{3,2,1,0:T(8,128)(2,1)S(1)} %get-tuple-element.15), channel_id=1, source_target_pairs={{0,48},{8,56},{16,32},{24,40},{32,16},{40,24},{48,0},{56,8},{64,11... | collective-permute-start | bytes 786440 | tf_op jit(solution)/shard_map/ppermute | solution.py:315
  37.5 12.3 %collective-permute-start.3 = (bf16[8,16,8,128]{3,2,1,0:T(8,128)(2,1)S(1)}, bf16[8,16,8,128]{3,2,1,0:T(8,128)(2,1)S(1)}, u32[]{:S(2)}, u32[]{:S(2)}) collective-permute-start(bf16[8,16,8,128]{3,2,1,0:T(8,128)(2,1)S(1)} %get-tuple-element.18), channel_id=1, source_target_pairs={{0,16},{8,24},{16,0},{24,8},{32,48},{40,56},{48,32},{56,40},{64,80... | collective-permute-start | bytes 786440 | tf_op jit(solution)/shard_map/ppermute | solution.py:315
  37.9 0.7 %copy-start = (s32[8]{0:T(128)S(1)}, s32[8]{0:T(128)}, u32[]{:S(2)}) copy-start(s32[8]{0:T(128)} %refs_1_.7) | copy-start | bytes 100
  42.1 10.5 %copy-start.1 = (s32[8]{0:T(128)S(1)}, s32[8]{0:T(128)}, u32[]{:S(2)}) copy-start(s32[8]{0:T(128)} %refs_1_.7) | copy-start | bytes 100
  49.8 2.0 %collective-permute-start.5 = (bf16[8,16,8,128]{3,2,1,0:T(8,128)(2,1)S(1)}, bf16[8,16,8,128]{3,2,1,0:T(8,128)(2,1)S(1)}, u32[]{:S(2)}, u32[]{:S(2)}) collective-permute-start(bf16[8,16,8,128]{3,2,1,0:T(8,128)(2,1)S(1)} %collective-permute-done.3.refs_4_), channel_id=1, source_target_pairs={{0,8},{8,0},{16,24},{24,16},{32,40},{40,32},{48,56},{56,48},{64,72... | collective-permute-start | bytes 786440 | tf_op jit(solution)/shard_map/ppermute | solution.py:315
  50.7 1.5 %collective-permute-start.6 = (bf16[8,16,8,128]{3,2,1,0:T(8,128)(2,1)S(1)}, bf16[8,16,8,128]{3,2,1,0:T(8,128)(2,1)S(1)}, u32[]{:S(2)}, u32[]{:S(2)}) collective-permute-start(bf16[8,16,8,128]{3,2,1,0:T(8,128)(2,1)S(1)} %collective-permute-done.4.refs_6_), channel_id=1, source_target_pairs={{0,8},{8,0},{16,24},{24,16},{32,40},{40,32},{48,56},{56,48},{64,72... | collective-permute-start | bytes 786440 | tf_op jit(solution)/shard_map/ppermute | solution.py:315
  50.7 1.9 %collective-permute-start.2 = (bf16[8,16,8,128]{3,2,1,0:T(8,128)(2,1)S(1)}, bf16[8,16,8,128]{3,2,1,0:T(8,128)(2,1)S(1)}, u32[]{:S(2)}, u32[]{:S(2)}) collective-permute-start(bf16[8,16,8,128]{3,2,1,0:T(8,128)(2,1)S(1)} %collective-permute-done.refs_3_), channel_id=1, source_target_pairs={{0,8},{8,0},{16,24},{24,16},{32,40},{40,32},{48,56},{56,48},{64,72... | collective-permute-start | bytes 786440 | tf_op jit(solution)/shard_map/ppermute | solution.py:315

commit v7 on v6

--- a/solution.py
+++ b/solution.py
@@ -328,8 +328,9 @@
     total = join(None, pairs=[(0 * core, own), (0 * core + 8, far), (1 + 6 * core, spare)])
     far_block, after = lax.optimization_barrier((moved[2], total))
     total = join(after, pairs=[(ahead[2], far_block)])
-    *near, total = lax.optimization_barrier((moved[1], moved[3], total))
-    pairs = [(ahead[2] + side, exchange(far_block, 1))]
+    passed = exchange(far_block, 1)
+    *near, passed, total = lax.optimization_barrier((moved[1], moved[3], passed, total))
+    pairs = [(ahead[2] + side, passed)]
     for flip, block in zip((1, 3), near):
         pairs += [(ahead[flip], block), (ahead[flip] + side, exchange(block, 1))]
     total = join(total, pairs=pairs)

time: 57.7 us -> 57.3 us (level)
  waiting for transfers between devices: 16.3 us -> 15.6 us
    ppermute x7, waiting for transfers between devices: 6.33 us -> 5.62 us  [exchange(): return lax.ppermute(array, 'stn', [(i, i ^ flip) for i in range(16)])]
  transfers between devices with their start and end apart: 8 -> 8, of which waited for: 7 -> 6; matrix products, arithmetic and copies ran while one was open for 0% -> 1% of each run, Pallas kernels for 11% -> 11%
where the time goes in v7:
time: 57.3 us; the launch traced here: 57.1 us
  Pallas kernels  24.2 us (42%)
  starting transfers between devices  16.2 us (28%)
  waiting for transfers between devices  15.6 us (27%)
  local copies, waits for them, and re-layouts  0.74 us (1%)
    pallas_call x1, Pallas kernels, channelize(): pl.pallas_call(channelize_kernel, in_specs=[hbm] * 5 + [vmem, pl.BlockSpe...  13.2 us
    pallas_call x3, Pallas kernels, correlate(): pl.pallas_call(functools.partial(correlate_kernel, count), in_specs=specs...  11 us
    all_to_all x1, waiting for transfers between devices, per_device(): lax.all_to_all(selected, ('stn', 'chan'), 0, 0, axis_index_groups=members...  9.94 us
    ppermute x7, starting transfers between devices, exchange(): return lax.ppermute(array, 'stn', [(i, i ^ flip) for i in range(16)])  8.61 us
    all_to_all x1, starting transfers between devices, per_device(): lax.all_to_all(selected, ('stn', 'chan'), 0, 0, axis_index_groups=members...  7.6 us
    ppermute x7, waiting for transfers between devices, exchange(): return lax.ppermute(array, 'stn', [(i, i ^ flip) for i in range(16)])  5.62 us
  transfers between devices with their start and end apart: 8, of which 6 were waited for; matrix products, arithmetic and copies ran while one was open for 1% of the time, Pallas kernels for 11%

profile of v7, /device:TPU:1, one launch (start us, length us, event | category | flops | bytes accessed | tf_op | source)
XLA Modules:
  0.0 57.1 jit_solution(8139352443528478796)
XLA Ops:
  0.0 13.2 %channelize.1 = bf16[2,8,16,8,128]{4,3,2,1,0:T(8,128)(2,1)} custom-call(bf16[2,31,8,8192]{3,2,1,0:T(8,128)(2,1)} %bitcast.20, f32[16,8192]{1,0:T(8,128)} %refs_1_.4, bf16[128,128]{1,0:T(8,128)(2,1)} %constant.91.clone.refs_2_, f32[2,64,128]{2,1,0:T(8,128)} %constant.93.clone.refs_3_, bf16[256,256]{1,0:T(8,128)(2,1)} %constant.92.clone.refs_4_, ...), custom_call_target="tpu_custom_call" | custom-call | tf_op jit(solution)/shard_map/channelize/pallas_call | solution.py:204
  13.2 7.6 %all-to-all-start = ((bf16[16,16,8,128]{3,2,1,0:T(8,128)(2,1)}), bf16[16,16,8,128]{3,2,1,0:T(8,128)(2,1)S(1)}, u32[]{:S(2)}, u32[]{:S(2)}) async-start(bf16[16,16,8,128]{3,2,1,0:T(8,128)(2,1)} %bitcast.21), calls=%async_computation | async-start | bytes 1048576 | tf_op jit(solution)/shard_map/all_to_all | solution.py:308
  20.9 9.9 %all-to-all-done = bf16[16,16,8,128]{3,2,1,0:T(8,128)(2,1)S(1)} async-done(((bf16[16,16,8,128]{3,2,1,0:T(8,128)(2,1)}), bf16[16,16,8,128]{3,2,1,0:T(8,128)(2,1)S(1)}, u32[]{:S(2)}, u32[]{:S(2)}) %all-to-all-start) | async-done | bytes 524320 | tf_op jit(solution)/shard_map/all_to_all | solution.py:308
  30.8 0.1 broadcast_select_fusion
  30.9 2.5 %collective-permute-start.3 = (bf16[8,16,8,128]{3,2,1,0:T(8,128)(2,1)S(1)}, bf16[8,16,8,128]{3,2,1,0:T(8,128)(2,1)S(1)}, u32[]{:S(2)}, u32[]{:S(2)}) collective-permute-start(bf16[8,16,8,128]{3,2,1,0:T(8,128)(2,1)S(1)} %get-tuple-element.17), channel_id=1, source_target_pairs={{0,8},{8,0},{16,24},{24,16},{32,40},{40,32},{48,56},{56,48},{64,72... | collective-permute-start | bytes 786440 | tf_op jit(solution)/shard_map/ppermute | solution.py:315
  33.4 0.1 broadcast_select_fusion.1
  33.4 3.7 %collective-permute-start.2 = (bf16[8,16,8,128]{3,2,1,0:T(8,128)(2,1)S(1)}, bf16[8,16,8,128]{3,2,1,0:T(8,128)(2,1)S(1)}, u32[]{:S(2)}, u32[]{:S(2)}) collective-permute-start(bf16[8,16,8,128]{3,2,1,0:T(8,128)(2,1)S(1)} %get-tuple-element.20), channel_id=1, source_target_pairs={{0,32},{8,40},{16,48},{24,56},{32,0},{40,8},{48,16},{56,24},{64,96... | collective-permute-start | bytes 786440 | tf_op jit(solution)/shard_map/ppermute | solution.py:315
  37.1 0.1 pad_add_fusion.refs_0_
  37.2 0.4 collective-permute-start.1
  37.6 0.4 collective-permute-start
  38.0 0.7 %copy-done = s32[8]{0:T(128)S(1)} copy-done((s32[8]{0:T(128)S(1)}, s32[8]{0:T(128)}, u32[]{:S(2)}) %copy-start) | copy-done | bytes 56
  38.7 3.5 %correlate.3.refs_4_ = f32[9,64,64,128]{3,2,1,0:T(8,128)} custom-call(s32[4]{0:T(128)S(1)} %pad_add_fusion.refs_0_, s32[8]{0:T(128)S(1)} %copy-done, bf16[8,16,8,128]{3,2,1,0:T(8,128)(2,1)S(1)} %get-tuple-element.19.refs_2_.refs_3_, bf16[8,16,8,128]{3,2,1,0:T(8,128)(2,1)S(1)} %get-tuple-element.19.refs_2_.refs_3_, ...), custom_call_target="tpu_custom_call" | custom-call | tf_op jit(solution)/shard_map/correlate/pallas_call | solution.py:283
  42.1 1.7 %collective-permute-done.2.refs_3_ = bf16[8,16,8,128]{3,2,1,0:T(8,128)(2,1)S(1)} collective-permute-done((bf16[8,16,8,128]{3,2,1,0:T(8,128)(2,1)S(1)}, bf16[8,16,8,128]{3,2,1,0:T(8,128)(2,1)S(1)}, u32[]{:S(2)}, u32[]{:S(2)}) %collective-permute-start.2) | collective-permute-done | bytes 262176 | tf_op jit(solution)/shard_map/ppermute | solution.py:315
  43.8 0.8 %collective-permute-start.4 = (bf16[8,16,8,128]{3,2,1,0:T(8,128)(2,1)S(1)}, bf16[8,16,8,128]{3,2,1,0:T(8,128)(2,1)S(1)}, u32[]{:S(2)}, u32[]{:S(2)}) collective-permute-start(bf16[8,16,8,128]{3,2,1,0:T(8,128)(2,1)S(1)} %collective-permute-done.2.refs_3_), channel_id=1, source_target_pairs={{0,8},{8,0},{16,24},{24,16},{32,40},{40,32},{48,56},{56,48},{64,72... | collective-permute-start | bytes 786440 | tf_op jit(solution)/shard_map/ppermute | solution.py:315
  44.6 0.1 pad_add_fusion.1.refs_0_
  44.7 2.7 %correlate.4.refs_8_ = f32[9,64,64,128]{3,2,1,0:T(8,128)} custom-call(s32[2]{0:T(128)S(1)} %pad_add_fusion.1.refs_0_, s32[8]{0:T(128)S(1)} %copy-done.1, bf16[8,16,8,128]{3,2,1,0:T(8,128)(2,1)S(1)} %get-tuple-element.19.refs_2_.refs_3_, bf16[8,16,8,128]{3,2,1,0:T(8,128)(2,1)S(1)} %collective-permute-done.2.refs_3_, ...), custom_call_target="tpu_custom_call", output_to_operand_aliasing={{}: (4, {})} | custom-call | tf_op jit(solution)/shard_map/correlate/pallas_call | solution.py:283
  47.4 2.1 %collective-permute-done.1.refs_6_ = bf16[8,16,8,128]{3,2,1,0:T(8,128)(2,1)S(1)} collective-permute-done((bf16[8,16,8,128]{3,2,1,0:T(8,128)(2,1)S(1)}, bf16[8,16,8,128]{3,2,1,0:T(8,128)(2,1)S(1)}, u32[]{:S(2)}, u32[]{:S(2)}) %collective-permute-start.1) | collective-permute-done | bytes 262176 | tf_op jit(solution)/shard_map/ppermute | solution.py:315
  49.5 0.4 collective-permute-done.refs_4_
  49.9 0.8 %collective-permute-start.5 = (bf16[8,16,8,128]{3,2,1,0:T(8,128)(2,1)S(1)}, bf16[8,16,8,128]{3,2,1,0:T(8,128)(2,1)S(1)}, u32[]{:S(2)}, u32[]{:S(2)}) collective-permute-start(bf16[8,16,8,128]{3,2,1,0:T(8,128)(2,1)S(1)} %collective-permute-done.refs_4_), channel_id=1, source_target_pairs={{0,8},{8,0},{16,24},{24,16},{32,40},{40,32},{48,56},{56,48},{64,72... | collective-permute-start | bytes 786440 | tf_op jit(solution)/shard_map/ppermute | solution.py:315
  50.8 0.0 collective-permute-start.6
  50.8 0.1 stack.41.refs_0_
  50.8 1.1 %collective-permute-done.5.refs_5_ = bf16[8,16,8,128]{3,2,1,0:T(8,128)(2,1)S(1)} collective-permute-done((bf16[8,16,8,128]{3,2,1,0:T(8,128)(2,1)S(1)}, bf16[8,16,8,128]{3,2,1,0:T(8,128)(2,1)S(1)}, u32[]{:S(2)}, u32[]{:S(2)}) %collective-permute-start.5) | collective-permute-done | bytes 262176 | tf_op jit(solution)/shard_map/ppermute | solution.py:315
  51.9 0.4 collective-permute-done.6.refs_7_
  52.3 4.8 %correlate.5 = f32[9,64,64,128]{3,2,1,0:T(8,128)} custom-call(s32[6]{0:T(128)S(1)} %stack.41.refs_0_, s32[8]{0:T(128)S(1)} %copy-done.1, bf16[8,16,8,128]{3,2,1,0:T(8,128)(2,1)S(1)} %get-tuple-element.19.refs_2_.refs_3_, bf16[8,16,8,128]{3,2,1,0:T(8,128)(2,1)S(1)} %collective-permute-done.4.refs_3_, ...), custom_call_target="tpu_custom_call", output_to_operand_aliasing={{}: (8, {})} | custom-call | tf_op jit(solution)/shard_map/correlate/pallas_call | solution.py:283
  (5 shorter events, 0.0 us)
Async XLA Ops:
  0.0 44.7 %copy-start.1 = (s32[8]{0:T(128)S(1)}, s32[8]{0:T(128)}, u32[]{:S(2)}) copy-start(s32[8]{0:T(128)} %refs_1_.7) | copy-start | bytes 100
  13.2 17.6 %all-to-all-start = ((bf16[16,16,8,128]{3,2,1,0:T(8,128)(2,1)}), bf16[16,16,8,128]{3,2,1,0:T(8,128)(2,1)S(1)}, u32[]{:S(2)}, u32[]{:S(2)}) async-start(bf16[16,16,8,128]{3,2,1,0:T(8,128)(2,1)} %bitcast.21), calls=%async_computation | async-start | bytes 1048576 | tf_op jit(solution)/shard_map/all_to_all | solution.py:308
  30.9 7.1 %collective-permute-start.3 = (bf16[8,16,8,128]{3,2,1,0:T(8,128)(2,1)S(1)}, bf16[8,16,8,128]{3,2,1,0:T(8,128)(2,1)S(1)}, u32[]{:S(2)}, u32[]{:S(2)}) collective-permute-start(bf16[8,16,8,128]{3,2,1,0:T(8,128)(2,1)S(1)} %get-tuple-element.17), channel_id=1, source_target_pairs={{0,8},{8,0},{16,24},{24,16},{32,40},{40,32},{48,56},{56,48},{64,72... | collective-permute-start | bytes 786440 | tf_op jit(solution)/shard_map/ppermute | solution.py:315
  33.4 10.4 %collective-permute-start.2 = (bf16[8,16,8,128]{3,2,1,0:T(8,128)(2,1)S(1)}, bf16[8,16,8,128]{3,2,1,0:T(8,128)(2,1)S(1)}, u32[]{:S(2)}, u32[]{:S(2)}) collective-permute-start(bf16[8,16,8,128]{3,2,1,0:T(8,128)(2,1)S(1)} %get-tuple-element.20), channel_id=1, source_target_pairs={{0,32},{8,40},{16,48},{24,56},{32,0},{40,8},{48,16},{56,24},{64,96... | collective-permute-start | bytes 786440 | tf_op jit(solution)/shard_map/ppermute | solution.py:315
  37.2 12.3 %collective-permute-start.1 = (bf16[8,16,8,128]{3,2,1,0:T(8,128)(2,1)S(1)}, bf16[8,16,8,128]{3,2,1,0:T(8,128)(2,1)S(1)}, u32[]{:S(2)}, u32[]{:S(2)}) collective-permute-start(bf16[8,16,8,128]{3,2,1,0:T(8,128)(2,1)S(1)} %get-tuple-element.21), channel_id=1, source_target_pairs={{0,48},{8,56},{16,32},{24,40},{32,16},{40,24},{48,0},{56,8},{64,11... | collective-permute-start | bytes 786440 | tf_op jit(solution)/shard_map/ppermute | solution.py:315
  37.6 12.3 %collective-permute-start = (bf16[8,16,8,128]{3,2,1,0:T(8,128)(2,1)S(1)}, bf16[8,16,8,128]{3,2,1,0:T(8,128)(2,1)S(1)}, u32[]{:S(2)}, u32[]{:S(2)}) collective-permute-start(bf16[8,16,8,128]{3,2,1,0:T(8,128)(2,1)S(1)} %get-tuple-element.22), channel_id=1, source_target_pairs={{0,16},{8,24},{16,0},{24,8},{32,48},{40,56},{48,32},{56,40},{64,80... | collective-permute-start | bytes 786440 | tf_op jit(solution)/shard_map/ppermute | solution.py:315
  38.0 0.7 %copy-start = (s32[8]{0:T(128)S(1)}, s32[8]{0:T(128)}, u32[]{:S(2)}) copy-start(s32[8]{0:T(128)} %refs_1_.7) | copy-start | bytes 100
  43.8 6.1 %collective-permute-start.4 = (bf16[8,16,8,128]{3,2,1,0:T(8,128)(2,1)S(1)}, bf16[8,16,8,128]{3,2,1,0:T(8,128)(2,1)S(1)}, u32[]{:S(2)}, u32[]{:S(2)}) collective-permute-start(bf16[8,16,8,128]{3,2,1,0:T(8,128)(2,1)S(1)} %collective-permute-done.2.refs_3_), channel_id=1, source_target_pairs={{0,8},{8,0},{16,24},{24,16},{32,40},{40,32},{48,56},{56,48},{64,72... | collective-permute-start | bytes 786440 | tf_op jit(solution)/shard_map/ppermute | solution.py:315
  49.9 2.0 %collective-permute-start.5 = (bf16[8,16,8,128]{3,2,1,0:T(8,128)(2,1)S(1)}, bf16[8,16,8,128]{3,2,1,0:T(8,128)(2,1)S(1)}, u32[]{:S(2)}, u32[]{:S(2)}) collective-permute-start(bf16[8,16,8,128]{3,2,1,0:T(8,128)(2,1)S(1)} %collective-permute-done.refs_4_), channel_id=1, source_target_pairs={{0,8},{8,0},{16,24},{24,16},{32,40},{40,32},{48,56},{56,48},{64,72... | collective-permute-start | bytes 786440 | tf_op jit(solution)/shard_map/ppermute | solution.py:315
  50.8 1.5 %collective-permute-start.6 = (bf16[8,16,8,128]{3,2,1,0:T(8,128)(2,1)S(1)}, bf16[8,16,8,128]{3,2,1,0:T(8,128)(2,1)S(1)}, u32[]{:S(2)}, u32[]{:S(2)}) collective-permute-start(bf16[8,16,8,128]{3,2,1,0:T(8,128)(2,1)S(1)} %collective-permute-done.1.refs_6_), channel_id=1, source_target_pairs={{0,8},{8,0},{16,24},{24,16},{32,40},{40,32},{48,56},{56,48},{64,72... | collective-permute-start | bytes 786440 | tf_op jit(solution)/shard_map/ppermute | solution.py:315
